TPU v7x, 32 devices: a whole 2x2x4 slice. The times are simulated.
32 devices in a mesh: dp: 8 (over z, x), row: 2 (over core), col: 2 (over y).
Axes of the slice: x: 2, y: 2, z: 4, core: 2. Of those that a mesh axis runs over, the one named last changes fastest.
Arguments:
- tokens: bfloat16 [128, 197, 768], P(('dp', 'row', 'col')), may hold values from -6 to 6
- cotangent: bfloat16 [128, 197, 768], P(('dp', 'row', 'col')), may hold values from -6 to 6
- triple_weight: bfloat16 [768, 3, 768], P('row', None, 'col'), may hold values from -0.3125 to 0.3125
- attend_bias: float32 [2, 768], P(None, 'col'), may hold values from -2 to 2
- merge_weight: bfloat16 [768, 768], P('col', 'row'), may hold values from -1.25 to 1.25
- expand_weight: bfloat16 [768, 3072], P('row', 'col'), may hold values from -0.21875 to 0.21875
- expand_bias: float32 [3072], P('col'), may hold values from -2 to 2
- shrink_weight: bfloat16 [3072, 768], P('col', 'row'), may hold values from -0.15625 to 0.15625
- norm_gain: float32 [2, 768], replicated, may hold values from 0.5 to 1.5
- norm_shift: float32 [2, 768], replicated, may hold values from -2 to 2
- branch_bias: float32 [2, 768], replicated, may hold values from -2 to 2
Outputs:
- block_out: bfloat16 [128, 197, 768], P(('dp', 'row', 'col'))
- tokens_grad: float32 [128, 197, 768], P(('dp', 'row', 'col'))
- triple_grad: float32 [768, 3, 768], P('row', None, 'col')
- attend_grad: float32 [2, 768], P(None, 'col')
- merge_grad: float32 [768, 768], P('col', 'row')
- expand_grad: float32 [768, 3072], P('row', 'col')
- hidden_grad: float32 [3072], P('col')
- shrink_grad: float32 [3072, 768], P('col', 'row')
- gain_grad: float32 [2, 768], replicated
- shift_grad: float32 [2, 768], replicated
- branch_grad: float32 [2, 768], replicated
All inputs are finite; a program needn't handle non-finite values.
Results may differ from a plain program's by a relative error of at most 0.012.
The roundings to bfloat16 on the way count: a program that leaves them out, or rounds other values in their place, can miss the bound.
Values may be sent and summed in bfloat16 or wider, within the bound.
A program may use at most 128 MiB of HBM per device.

v0:
```python
import jax
import jax.numpy as jnp
from jax import lax
from jax.sharding import PartitionSpec as P

HEAD_DIM = 64


EPSILON = 1e-06


def gelu_exact(source):
    return jax.nn.gelu(source, approximate=False)


def normalize(source, norm_scale, norm_offset):
    average = jnp.mean(source, axis=-1, keepdims=True)
    variance = jnp.mean(source * source, axis=-1, keepdims=True) - average * average
    inverse = lax.rsqrt(variance + EPSILON)
    unit_rows = (source - average) * inverse
    return (unit_rows * norm_scale + norm_offset, unit_rows, inverse)


def norm_backward(grad_output, unit_rows, inverse, norm_scale):
    scaled = grad_output * norm_scale
    centred = scaled - jnp.mean(scaled, axis=-1, keepdims=True)
    return inverse * (centred - unit_rows * jnp.mean(scaled * unit_rows, axis=-1, keepdims=True))


def gather_images(source):
    return lax.all_gather(source, "col", axis=0, tiled=True)


def gather_grads(source):
    return lax.all_gather(source, "col", axis=0, tiled=True)


def branch_total(source, matrix, pattern):
    return lax.psum_scatter(
        jnp.einsum(pattern, source, matrix, preferred_element_type=jnp.float32),
        "col",
        scatter_dimension=0,
        tiled=True,
    )


def normed_total(source, matrix, pattern):
    return lax.psum_scatter(
        jnp.einsum(pattern, source, matrix, preferred_element_type=jnp.float32),
        "col",
        scatter_dimension=0,
        tiled=True,
    )


def on_device(
    tokens,
    cotangent,
    triple_weight,
    attend_bias,
    merge_weight,
    expand_weight,
    expand_bias,
    shrink_weight,
    norm_gain,
    norm_shift,
    branch_bias,
):
    triple_full, merge_full, expand_full, shrink_full = (
        lax.all_gather(triple_weight, "row", axis=0, tiled=True),
        lax.all_gather(merge_weight, "row", axis=1, tiled=True),
        lax.all_gather(expand_weight, "row", axis=0, tiled=True),
        lax.all_gather(shrink_weight, "row", axis=1, tiled=True),
    )
    scale_factor = HEAD_DIM ** (-0.5)
    inputs = tokens.astype(jnp.float32)
    shaped_one, unit_one, inverse_one = normalize(inputs, norm_gain[0], norm_shift[0])
    normed_one = gather_images(shaped_one.astype(jnp.bfloat16))
    group_rows = normed_one.shape[0]
    seq_length = normed_one.shape[1]
    projected = jnp.einsum(
        "nsd,dte->nste", normed_one, triple_full, preferred_element_type=jnp.float32
    )
    queries = (projected[:, :, 0] + attend_bias[0]).astype(jnp.bfloat16)
    key_rows = projected[:, :, 1].astype(jnp.bfloat16)
    value_rows = (projected[:, :, 2] + attend_bias[1]).astype(jnp.bfloat16)
    heads_local = queries.shape[-1] // HEAD_DIM

    def to_heads(source):
        return source.reshape(source.shape[0], source.shape[1], heads_local, HEAD_DIM)

    def score_rows():
        return (
            jnp.einsum(
                "nqhe,nkhe->nhqk",
                to_heads(queries),
                to_heads(key_rows),
                preferred_element_type=jnp.float32,
            )
            * scale_factor
        )

    logits = score_rows()
    log_total = jax.nn.logsumexp(logits, axis=-1, keepdims=True)
    weights = jnp.exp(logits - log_total).astype(jnp.bfloat16)
    attended = jnp.einsum(
        "nhqk,nkhe->nqhe", weights, to_heads(value_rows), preferred_element_type=jnp.float32
    )
    attended = attended.reshape(group_rows, seq_length, heads_local * HEAD_DIM).astype(jnp.bfloat16)
    branch_one = branch_total(attended, merge_full, "nse,ed->nsd")
    middle = inputs + branch_one + branch_bias[0]
    shaped_two, unit_two, inverse_two = normalize(middle, norm_gain[1], norm_shift[1])
    normed_two = gather_images(shaped_two.astype(jnp.bfloat16))
    hidden = (
        jnp.einsum("nsd,df->nsf", normed_two, expand_full, preferred_element_type=jnp.float32)
        + expand_bias
    )
    active = gelu_exact(hidden).astype(jnp.bfloat16)
    branch_two = branch_total(active, shrink_full, "nsf,fd->nsd")
    block_out = (middle + branch_two + branch_bias[1]).astype(jnp.bfloat16)
    grad_out = cotangent.astype(jnp.float32)
    grad_two = gather_grads(grad_out.astype(jnp.bfloat16))
    shrink_part = jnp.einsum("nsf,nsd->fd", active, grad_two, preferred_element_type=jnp.float32)
    grad_active = jnp.einsum(
        "nsd,fd->nsf", grad_two, shrink_full, preferred_element_type=jnp.float32
    )
    gelu_value, gelu_pull = jax.vjp(gelu_exact, hidden)
    grad_hidden = gelu_pull(grad_active)[0].astype(jnp.bfloat16)
    hidden_part = jnp.sum(grad_hidden.astype(jnp.float32), axis=(0, 1))
    expand_part = jnp.einsum(
        "nsd,nsf->df", normed_two, grad_hidden, preferred_element_type=jnp.float32
    )
    grad_normed_two = normed_total(grad_hidden, expand_full, "nsf,df->nsd")
    gain_two = jnp.sum(grad_normed_two * unit_two, axis=(0, 1))
    shift_two = jnp.sum(grad_normed_two, axis=(0, 1))
    grad_middle = grad_out + norm_backward(grad_normed_two, unit_two, inverse_two, norm_gain[1])
    grad_one = gather_grads(grad_middle.astype(jnp.bfloat16))
    merge_part = jnp.einsum("nse,nsd->ed", attended, grad_one, preferred_element_type=jnp.float32)
    grad_attended = jnp.einsum(
        "nsd,ed->nse", grad_one, merge_full, preferred_element_type=jnp.float32
    ).astype(jnp.bfloat16)
    grad_heads = to_heads(grad_attended)
    probs = jnp.exp(score_rows() - log_total)
    grad_probs = jnp.einsum(
        "nqhe,nkhe->nhqk", grad_heads, to_heads(value_rows), preferred_element_type=jnp.float32
    )
    grad_logits = (
        probs * (grad_probs - jnp.sum(probs * grad_probs, axis=-1, keepdims=True)) * scale_factor
    ).astype(jnp.bfloat16)
    grad_queries = jnp.einsum(
        "nhqk,nkhe->nqhe", grad_logits, to_heads(key_rows), preferred_element_type=jnp.float32
    )
    grad_keys = jnp.einsum(
        "nhqk,nqhe->nkhe", grad_logits, to_heads(queries), preferred_element_type=jnp.float32
    )
    grad_values = jnp.einsum(
        "nhqk,nqhe->nkhe",
        probs.astype(jnp.bfloat16),
        grad_heads,
        preferred_element_type=jnp.float32,
    )
    flat_shape = (group_rows, seq_length, heads_local * HEAD_DIM)
    grad_triple = jnp.stack(
        [
            grad_queries.reshape(flat_shape),
            grad_keys.reshape(flat_shape),
            grad_values.reshape(flat_shape),
        ],
        axis=2,
    ).astype(jnp.bfloat16)
    attend_part = jnp.sum(grad_triple.astype(jnp.float32), axis=(0, 1))[jnp.array([0, 2])]
    triple_part = jnp.einsum(
        "nsd,nste->dte", normed_one, grad_triple, preferred_element_type=jnp.float32
    )
    grad_normed_one = normed_total(grad_triple, triple_full, "nste,dte->nsd")
    gain_one = jnp.sum(grad_normed_one * unit_one, axis=(0, 1))
    shift_one = jnp.sum(grad_normed_one, axis=(0, 1))
    tokens_grad = grad_middle + norm_backward(grad_normed_one, unit_one, inverse_one, norm_gain[0])
    shared = jnp.stack(
        [
            gain_one,
            gain_two,
            shift_one,
            shift_two,
            jnp.sum(grad_middle, axis=(0, 1)),
            jnp.sum(grad_out, axis=(0, 1)),
        ]
    )
    shared = lax.psum(shared, ("dp", "row", "col"))
    attend_grad, hidden_grad = lax.psum((attend_part, hidden_part), ("dp", "row"))
    summed = lax.psum((triple_part, merge_part, expand_part, shrink_part), "dp")
    triple_grad, merge_grad, expand_grad, shrink_grad = (
        lax.psum_scatter(summed[0], "row", scatter_dimension=0, tiled=True),
        lax.psum_scatter(summed[1], "row", scatter_dimension=1, tiled=True),
        lax.psum_scatter(summed[2], "row", scatter_dimension=0, tiled=True),
        lax.psum_scatter(summed[3], "row", scatter_dimension=1, tiled=True),
    )
    return (
        block_out,
        tokens_grad,
        triple_grad,
        attend_grad,
        merge_grad,
        expand_grad,
        hidden_grad,
        shrink_grad,
        shared[0:2],
        shared[2:4],
        shared[4:6],
    )


def solution(mesh):
    placed = (
        P(("dp", "row", "col"), None, None),
        P(("dp", "row", "col"), None, None),
        P("row", None, "col"),
        P(None, "col"),
        P("col", "row"),
        P("row", "col"),
        P("col"),
        P("col", "row"),
        P(),
        P(),
        P(),
    )
    return jax.shard_map(
        on_device,
        mesh=mesh,
        in_specs=placed,
        out_specs=(
            P(("dp", "row", "col"), None, None),
            P(("dp", "row", "col"), None, None),
            P("row", None, "col"),
            P(None, "col"),
            P("col", "row"),
            P("row", "col"),
            P("col"),
            P("col", "row"),
            P(),
            P(),
            P(),
        ),
        check_vma=False,
    )
```

profile of v0, /device:TPU:0, one launch (start us, length us, event | category | flops | bytes accessed | tf_op | source)
XLA Modules:
  0.0 864.8 jit_solution(9802521014260418402)
XLA Ops:
  11.9 2.8 fusion.31
  15.0 2.4 all_gather.26
  17.4 5.0 all-gather.10.cloned.1.call-done
  22.4 40.5 %all-gather.8.cloned.1.call-done = bf16[8,197,768]{2,1,0:T(8,128)(2,1)} async-done(((bf16[4,197,768]{2,1,0:T(8,128)(2,1)}), bf16[8,197,768]{2,1,0:T(8,128)(2,1)}) %all-gather.8.cloned.1.call-update) | async-done | bytes 2420752 | tf_op jit(solution)/shard_map/all_gather | solution.py:31
  62.9 5.6 fusion.41
  68.6 2.5 fusion.82
  74.5 3.3 copy.66
  77.9 3.2 multiply_reduce_fusion.1
  87.2 7.0 convolution_convert_fusion.1
  95.3 3.8 fusion.68
  100.0 61.4 %reduce-scatter.9.cloned.1.call-done = f32[4,197,768]{2,1,0:T(8,128)} async-done(((f32[8,197,768]{2,1,0:T(8,128)}), f32[4,197,768]{2,1,0:T(8,128)}) %reduce-scatter.9.cloned.1.call-update) | async-done | bytes 2420752 | tf_op jit(solution)/shard_map/reduce_scatter | solution.py:39
  161.4 2.6 fusion.78
  166.1 2.4 copy.69
  168.6 5.2 all-gather.14.cloned.1.call-done
  173.8 40.3 %all-gather.12.cloned.1.call-done = bf16[8,197,768]{2,1,0:T(8,128)(2,1)} async-done(((bf16[4,197,768]{2,1,0:T(8,128)(2,1)}), bf16[8,197,768]{2,1,0:T(8,128)(2,1)}) %all-gather.12.cloned.1.call-update) | async-done | bytes 2420752 | tf_op jit(solution)/shard_map/all_gather | solution.py:31
  214.2 9.3 %fusion.44 = (u8[197,1536]{1,0:T(8,128)(4,1)S(1)}, u8[197,1536]{1,0:T(8,128)(4,1)S(1)}, f32[8,197,1536]{2,1,0:T(8,128)S(1)}) fusion(f32[1536]{0:T(1024)S(1)} %copy-done.24, bf16[8,197,768]{2,1,0:T(8,128)(2,1)} %all-gather.12.cloned.1.call-done, bf16[768,1536]{1,0:T(8,128)(2,1)} %all-gather.14.cloned.1.call-done), kind=kOutput, calls=%fused_computation.75 | convolution fusion | flops 3751535616 | bytes 15074304 | tf_op jit(solution)/shard_map/nsd,df->nsf/dot_general | solution.py:115
  223.5 3.7 copy-done.9
  227.2 24.2 %multiply_convert_fusion.1 = (bf16[8,197,1536]{2,1,0:T(8,128)(2,1)}, f32[8,197,1536]{2,1,0:T(8,128)}) fusion(f32[8,197,1536]{2,1,0:T(8,128)S(1)} %get-tuple-element.90, f32[1536]{0:T(1024)S(1)} %copy-done.24, u8[197,1536]{1,0:T(8,128)(4,1)S(1)} %get-tuple-element.45, u8[197,1536]{1,0:T(8,128)(4,1)S(1)} %get-tuple-element.44), kind=kLoop, calls=%fused_computation.14 | loop fusion | flops 171872256 | bytes 24818688 | tf_op jit(solution)/shard_map/convert_element_type | solution.py:118
  251.3 15.7 %all-gather.18.cloned.1.call-done = bf16[8,197,768]{2,1,0:T(8,128)(2,1)} async-done(((bf16[4,197,768]{2,1,0:T(8,128)(2,1)}), bf16[8,197,768]{2,1,0:T(8,128)(2,1)}) %all-gather.18.cloned.1.call-update) | async-done | bytes 2420752 | tf_op jit(solution)/shard_map/all_gather | solution.py:35
  267.0 14.0 %convert_reduce_fusion = (f32[1536]{0:T(1024)S(1)}, bf16[8,197,1536]{2,1,0:T(8,128)(2,1)S(1)}) fusion(f32[8,197,1536]{2,1,0:T(8,128)} %get-tuple-element.75, bf16[8,197,768]{2,1,0:T(8,128)(2,1)} %all-gather.18.cloned.1.call-done, bf16[1536,768]{1,0:T(8,128)(2,1)} %all-gather.16.cloned.1.call-done, f32[8,197,1536]{2,1,0:T(8,128)} %copy-done.9, ...), kind=kOutput, calls=%fused_computation.9 | convolution fusion | flops 3759401472 | bytes 28999680 | tf_op jit(solution)/shard_map/nsd,fd->nsf/dot_general | solution.py:124
  281.0 2.3 copy-done.30
  283.3 5.7 fusion.48
  289.1 9.4 %fusion.46 = f32[8,197,768]{2,1,0:T(8,128)} fusion(bf16[8,197,1536]{2,1,0:T(8,128)(2,1)} %get-tuple-element.74, bf16[1536,768]{1,0:T(8,128)(2,1)} %all-gather.16.cloned.1.call-done), kind=kOutput, calls=%fused_computation.77 | convolution fusion | flops 3718250496 | bytes 12042240 | tf_op jit(solution)/shard_map/nsf,fd->nsd/dot_general | solution.py:40
  298.6 52.7 %reduce-scatter.13.cloned.1.call-done = f32[4,197,768]{2,1,0:T(8,128)} async-done(((f32[8,197,768]{2,1,0:T(8,128)}), f32[4,197,768]{2,1,0:T(8,128)}) %reduce-scatter.13.cloned.1.call-update) | async-done | bytes 2420752 | tf_op jit(solution)/shard_map/reduce_scatter | solution.py:48
  351.3 2.8 multiply_reduce_fusion.2
  354.1 61.7 %reduce-scatter.11.cloned.1.call-done = f32[4,197,768]{2,1,0:T(8,128)} async-done(((f32[8,197,768]{2,1,0:T(8,128)}), f32[4,197,768]{2,1,0:T(8,128)}) %reduce-scatter.11.cloned.1.call-update) | async-done | bytes 2420752 | tf_op jit(solution)/shard_map/reduce_scatter | solution.py:39
  415.8 4.3 fusion.79
  422.9 8.7 %convolution_bitcast_fusion.1 = f32[768,1536]{1,0:T(8,128)} fusion(bf16[8,197,768]{2,1,0:T(8,128)(2,1)S(1)} %copy-done.27, bf16[8,197,1536]{2,1,0:T(8,128)(2,1)} %copy-done.30), kind=kOutput, calls=%fused_computation.43 | convolution fusion | flops 3718250496 | bytes 11980800 | tf_op jit(solution)/shard_map/nsd,nsf->df/dot_general | solution.py:130
  433.5 9.1 %convolution_bitcast_fusion = f32[1536,768]{1,0:T(8,128)} fusion(bf16[8,197,1536]{2,1,0:T(8,128)(2,1)} %get-tuple-element.74, bf16[8,197,768]{2,1,0:T(8,128)(2,1)S(1)} %copy-done.28), kind=kOutput, calls=%fused_computation.42 | convolution fusion | flops 3718250496 | bytes 11980800 | tf_op jit(solution)/shard_map/nsf,nsd->fd/dot_general | solution.py:123
  442.7 17.4 %all-gather.20.cloned.1.call-done = bf16[8,197,768]{2,1,0:T(8,128)(2,1)} async-done(((bf16[4,197,768]{2,1,0:T(8,128)(2,1)}), bf16[8,197,768]{2,1,0:T(8,128)(2,1)}) %all-gather.20.cloned.1.call-update) | async-done | bytes 2420752 | tf_op jit(solution)/shard_map/all_gather | solution.py:35
  460.1 3.2 convolution_convert_fusion.2
  464.8 4.6 convolution_bitcast_fusion.3
  469.5 6.9 fusion.65
  476.5 19.1 %fusion.57 = bf16[8,6,64,197]{3,2,1,0:T(8,128)(2,1)} fusion(bf16[8,197,6,64]{1,3,2,0:T(8,128)(2,1)} %bitcast.91, f32[8,6,197,197]{2,3,1,0:T(8,128)} %fusion.65, f32[8,6,197,197]{2,3,1,0:T(8,128)} %copy-done, f32[8,6,197]{2,1,0:T(8,128)S(1)} %log_add_fusion), kind=kOutput, calls=%fused_computation.89 | convolution fusion | flops 255822816 | bytes 17361216 | tf_op jit(solution)/shard_map/nhqk,nkhe->nqhe/dot_general | solution.py:150
  495.6 2.5 copy.75
  498.1 16.5 %fusion.60 = bf16[8,6,64,197]{3,2,1,0:T(8,128)(2,1)} fusion(f32[8,6,197,197]{2,3,1,0:T(8,128)} %fusion.65, f32[8,6,197,197]{2,3,1,0:T(8,128)} %copy-done, f32[8,6,197]{2,1,0:T(8,128)S(1)} %log_add_fusion, f32[8,197,6,64]{1,3,2,0:T(8,128)S(1)} %bitcast.86, f32[6,64]{1,0:T(8,128)S(1)} %add.146), kind=kOutput, calls=%fused_computation.90 | convolution fusion | flops 257033184 | bytes 18573120 | tf_op jit(solution)/shard_map/nhqk,nqhe->nkhe/dot_general | solution.py:153
  514.6 2.6 copy.76
  517.3 5.7 convolution_convert_fusion
  524.5 8.4 fusion.52
  533.2 7.9 convolution_bitcast_fusion.2
  541.2 3.4 reduce-scatter.17.cloned.1.call-done
  544.8 2.9 copy.80
  550.1 61.9 %all-reduce = (f32[2,384]{1,0:T(2,128)}, f32[1536]{0:T(1024)}) all-reduce(f32[2,384]{1,0:T(2,128)S(1)} %gather_fusion, f32[1536]{0:T(1024)S(1)} %get-tuple-element.91), channel_id=1, replica_groups=mesh['dp'=8,'row'=2,'col'=2] {'dp','row'}, use_global_device_ids=true, to_apply=%region_18.0 | all-reduce | flops 2304 | bytes 18432 | tf_op jit(solution)/shard_map/psum | solution.py:190
  612.0 3.0 fusion.36
  617.4 2.4 copy.81
  619.8 41.1 %psum.55 = f32[6,768]{1,0:T(8,128)S(1)} all-reduce(f32[6,768]{1,0:T(8,128)S(1)} %stack.32), channel_id=1, replica_groups=mesh['dp'=8,'row'=2,'col'=2] {'dp','row','col'}, use_global_device_ids=true, to_apply=%region_33.0 | all-reduce | flops 4608 | bytes 36864 | tf_op jit(solution)/shard_map/psum | solution.py:189
  661.5 189.7 %all-reduce.4.cloned.1.call-done = (f32[384,3,384]{2,0,1:T(8,128)}, f32[384,384]{1,0:T(8,128)}, f32[384,1536]{1,0:T(8,128)}, f32[1536,384]{1,0:T(8,128)}) async-done(((f32[384,3,384]{2,0,1:T(8,128)}, f32[384,384]{1,0:T(8,128)}, f32[384,1536]{1,0:T(8,128)}, f32[1536,384]{1,0:T(8,128)}), (f32[384,3,384]{2,0,1:T(8,128)}, f32[384,384]{1,0:T(8,128)}, f32[384,1536]{1,0:T(8,128)}, ...) | async-done | bytes 7077904 | tf_op jit(solution)/shard_map/psum | solution.py:191
  851.2 2.9 copy.106
  (135 shorter events, 36.2 us)
Async XLA Ops:
  7.2 7.7 copy-start.26
  7.2 7.8 copy-start.17
  7.2 15.2 %all-gather.10.cloned.1.call-start = ((), (), s32[]{:S(2)}) async-start(), calls=%async_computation.9 | async-start | bytes 2654208 | tf_op jit(solution)/shard_map/all_gather | solution.py:70
  7.9 55.0 %all-gather.8.cloned.1.call-start = ((), (), s32[]{:S(2)}) async-start(), calls=%async_computation.8 | async-start | bytes 3686400 | tf_op jit(solution)/shard_map/all_gather | solution.py:31
  8.8 2.6 copy-start.18
  11.3 0.6 copy-start.20
  11.3 0.6 copy-start.22
  14.8 146.6 %reduce-scatter.9.cloned.1.call-start = ((), (), s32[]{:S(2)}) async-start(), calls=%async_computation.10 | async-start | bytes 7372800 | tf_op jit(solution)/shard_map/reduce_scatter | solution.py:39
  74.5 6.5 copy-start.7
  81.1 3.8 copy-start
  87.1 7.0 copy-start.2
  87.1 8.2 copy-start.12
  94.2 1.1 copy-start.10
  99.1 0.9 copy-start.25
  99.1 74.7 %all-gather.14.cloned.1.call-start = ((), (), s32[]{:S(2)}) async-start(), calls=%async_computation.12 | async-start | bytes 3538944 | tf_op jit(solution)/shard_map/all_gather | solution.py:72
  99.7 114.5 %all-gather.12.cloned.1.call-start = ((), (), s32[]{:S(2)}) async-start(), calls=%async_computation.11 | async-start | bytes 3686400 | tf_op jit(solution)/shard_map/all_gather | solution.py:31
  165.4 48.7 %copy-start.24 = (f32[1536]{0:T(1024)S(1)}, f32[1536]{0:T(1024)}, u32[]{:S(2)}) copy-start(f32[1536]{0:T(1024)} %param.18) | copy-start | bytes 18436
  165.5 85.9 %all-gather.16.cloned.1.call-start = ((), (), s32[]{:S(2)}) async-start(), calls=%async_computation.13 | async-start | bytes 3538944 | tf_op jit(solution)/shard_map/all_gather | solution.py:73
  166.0 101.0 %all-gather.18.cloned.1.call-start = ((), (), s32[]{:S(2)}) async-start(), calls=%async_computation.15 | async-start | bytes 3686400 | tf_op jit(solution)/shard_map/all_gather | solution.py:35
  168.5 182.7 %reduce-scatter.13.cloned.1.call-start = ((), (), s32[]{:S(2)}) async-start(), calls=%async_computation.16 | async-start | bytes 7372800 | tf_op jit(solution)/shard_map/reduce_scatter | solution.py:48
  223.4 3.7 copy-start.9
  267.0 16.3 %copy-start.29 = (bf16[768,1536]{1,0:T(8,128)(2,1)S(1)}, bf16[768,1536]{1,0:T(8,128)(2,1)}, u32[]{:S(2)}) copy-start(bf16[768,1536]{1,0:T(8,128)(2,1)} %all-gather.14.cloned.1.call-done) | copy-start | bytes 7077892
  281.0 2.3 copy-start.30
  289.0 126.8 %reduce-scatter.11.cloned.1.call-start = ((), (), s32[]{:S(2)}) async-start(), calls=%async_computation.14 | async-start | bytes 7372800 | tf_op jit(solution)/shard_map/reduce_scatter | solution.py:39
  298.5 161.5 %all-gather.20.cloned.1.call-start = ((), (), s32[]{:S(2)}) async-start(), calls=%async_computation.17 | async-start | bytes 3686400 | tf_op jit(solution)/shard_map/all_gather | solution.py:35
  420.1 1.4 copy-start.4
  420.1 2.8 copy-start.27
  422.7 118.5 %reduce-scatter.21.cloned.1.call-start = ((), (), s32[]{:S(2)}) async-start(), calls=%async_computation.21 | async-start | bytes 7077888 | tf_op jit(solution)/shard_map/reduce_scatter | solution.py:195
  431.6 1.9 copy-start.28
  431.6 109.6 %reduce-scatter.23.cloned.1.call-start = ((), (), s32[]{:S(2)}) async-start(), calls=%async_computation.22 | async-start | bytes 7077888 | tf_op jit(solution)/shard_map/reduce_scatter | solution.py:196
  442.6 17.5 %copy-start.13 = (bf16[384,768]{1,0:T(8,128)(2,1)S(1)}, bf16[384,768]{1,0:T(8,128)(2,1)}, u32[]{:S(2)}) copy-start(bf16[384,768]{1,0:T(8,128)(2,1)} %all_gather.26) | copy-start | bytes 1769476
  442.6 98.6 %reduce-scatter.19.cloned.1.call-start = ((), (), s32[]{:S(2)}) async-start(), calls=%async_computation.20 | async-start | bytes 1769472 | tf_op jit(solution)/shard_map/reduce_scatter | solution.py:194
  464.8 4.7 copy-start.3
  469.5 75.2 %reduce-scatter.17.cloned.1.call-start = ((), (), s32[]{:S(2)}) async-start(), calls=%async_computation.19 | async-start | bytes 5308416 | tf_op jit(solution)/shard_map/reduce_scatter | solution.py:193
  476.4 21.7 %copy-start.8 = (f32[8,197,1,384]{1,3,0,2:T(8,128)S(1)}, f32[8,197,1,384]{1,3,0,2:T(8,128)}, u32[]{:S(2)}) copy-start(f32[8,197,1,384]{1,3,0,2:T(8,128)} %copy-done.7) | copy-start | bytes 7262212
  514.6 2.6 copy-start.6
  524.5 8.7 %copy-start.11 = (bf16[8,197,1,384]{3,1,2,0:T(8,128)(2,1)S(1)}, bf16[8,197,1,384]{3,1,2,0:T(8,128)(2,1)}, u32[]{:S(2)}) copy-start(bf16[8,197,1,384]{3,1,2,0:T(8,128)(2,1)} %copy.75) | copy-start | bytes 3631108
  532.9 79.1 %reduce-scatter.15.cloned.1.call-start = ((), (), s32[]{:S(2)}) async-start(), calls=%async_computation.18 | async-start | bytes 7372800 | tf_op jit(solution)/shard_map/reduce_scatter | solution.py:48
  541.1 310.1 %all-reduce.4.cloned.1.call-start = ((), (), s32[]{:S(2)}) async-start(), calls=%async_computation.23 | async-start | bytes 14155776 | tf_op jit(solution)/shard_map/psum | solution.py:191
  544.6 67.3 %copy-start.1 = (bf16[4,197,768]{2,0,1:T(4,128)(2,1)S(1)}, bf16[4,197,768]{2,0,1:T(4,128)(2,1)}, u32[]{:S(2)}) copy-start(bf16[4,197,768]{2,0,1:T(4,128)(2,1)} %param.12) | copy-start | bytes 3631108
  544.7 67.3 %copy-start.19 = (f32[768]{0:T(1024)S(1)}, f32[768]{0:T(1024)}, u32[]{:S(2)}) copy-start(f32[768]{0:T(1024)} %copy-done.18) | copy-start | bytes 9220
  544.7 67.3 %copy-start.21 = (f32[4,197]{1,0:T(4,128)S(1)}, f32[4,197]{1,0:T(4,128)}, u32[]{:S(2)}) copy-start(f32[4,197]{1,0:T(4,128)} %copy-done.20) | copy-start | bytes 9460
  544.7 67.3 %copy-start.23 = (f32[4,197]{1,0:T(4,128)S(1)}, f32[4,197]{1,0:T(4,128)}, u32[]{:S(2)}) copy-start(f32[4,197]{1,0:T(4,128)} %copy-done.22) | copy-start | bytes 9460
  612.0 3.1 copy-start.5
  851.2 3.0 copy-start.16
  851.2 3.8 copy-start.15
  854.2 2.2 copy-start.14
Sparse Core Ops, SparseCore 0:
  9.6 12.7 all-gather.9
  24.5 38.3 all-gather.7
  99.2 62.0 reduce-scatter.8
  162.8 10.9 all-gather.13
  175.8 38.3 all-gather.11
  215.5 10.8 all-gather.15
  228.6 38.3 all-gather.17
  289.1 62.0 reduce-scatter.12
  353.6 62.1 reduce-scatter.10
  422.8 37.1 all-gather.19
  462.4 12.6 reduce-scatter.20
  477.3 13.7 reduce-scatter.22
  493.9 9.8 reduce-scatter.18
  533.0 11.5 reduce-scatter.16
  546.8 63.2 reduce-scatter.14
  614.4 236.8 all-reduce.3
where the time goes:
time: 875 us; the launch traced here: 865 us
  waiting for transfers between devices  495 us (57%)
  matrix products  148 us (17%)
  blocking collectives  105 us (12%)
  other arithmetic  50.4 us (6%)
  local copies, waits for them, and re-layouts  50 us (6%)
  between operations  14.9 us (2%)
    psum x1, waiting for transfers between devices, on_device(): summed = lax.psum((triple_part, merge_part, expand_part, shrink_part), 'dp')  190 us
    reduce_scatter x2, waiting for transfers between devices, branch_total(): lax.psum_scatter(jnp.einsum(pattern, source, matrix, preferred_element_ty...  123 us
    all_gather x2, waiting for transfers between devices, gather_images(): return lax.all_gather(source, 'col', axis=0, tiled=True)  80.8 us
    psum x1, blocking collectives, on_device(): lax.psum((attend_part, hidden_part), ('dp', 'row'))  61.9 us
    reduce_scatter x2, waiting for transfers between devices, normed_total(): lax.psum_scatter(jnp.einsum(pattern, source, matrix, preferred_element_ty...  52.7 us
    psum x1, blocking collectives, on_device(): shared = lax.psum(shared, ('dp', 'row', 'col'))  41.1 us
    all_gather x2, waiting for transfers between devices, gather_grads(): return lax.all_gather(source, 'col', axis=0, tiled=True)  33.1 us
    unnamed x69, local copies, waits for them, and re-layouts  27.2 us
  transfers between devices with their start and end apart: 16, of which 11 were waited for; matrix products, arithmetic and copies ran while one was open for 20% of the time, Pallas kernels for 0%

commit v1 on v0

v1 whole, which is shorter than its diff:
```python
import functools
import math

import jax
import jax.numpy as jnp
from jax import lax
from jax.experimental import pallas as pl
from jax.experimental.pallas import tpu as pltpu
from jax.sharding import PartitionSpec as P

HEAD_DIM = 64
EPSILON = 1e-06
F32 = jnp.float32
BF16 = jnp.bfloat16
VMEM_BYTES = 56 * 1024 * 1024


def mean_rows(source):
    return jnp.mean(source, axis=-1, keepdims=True)


def unit_norm(source):
    average = mean_rows(source)
    variance = mean_rows(source * source) - average * average
    inverse = lax.rsqrt(variance + EPSILON)
    return (source - average) * inverse, inverse


def norm_backward(grad, unit, inverse, gain):
    scaled = grad * gain
    return inverse * (scaled - mean_rows(scaled) - unit * mean_rows(scaled * unit))


def dot(left, right):
    return jnp.dot(left, right, preferred_element_type=F32)


def dot_rows(left, right):
    return lax.dot_general(left, right, (((1,), (1,)), ((), ())), preferred_element_type=F32)


def dot_tokens(left, right):
    return lax.dot_general(left, right, (((0,), (0,)), ((), ())), preferred_element_type=F32)


def column_sum(source):
    return jnp.sum(source, axis=0, keepdims=True)


def assemble_triple(blocks_ref, full_ref, width):
    row_count, col_count, _, depth, cols = blocks_ref.shape
    for r in range(row_count):
        for c in range(col_count):
            for t in range(3):
                full_ref[r * depth : (r + 1) * depth, t * width + c * cols : t * width + (c + 1) * cols] = (
                    blocks_ref[r, c, t]
                )


def assemble_merge(blocks_ref, full_ref):
    row_count, col_count, depth, cols = blocks_ref.shape
    for r in range(row_count):
        for c in range(col_count):
            full_ref[c * depth : (c + 1) * depth, r * cols : (r + 1) * cols] = blocks_ref[r, c]


def attend_kernel(seq, x_ref, triple_ref, merge_ref, vec_ref, qkv_ref, attended_ref, middle_ref, triple_full, merge_full):
    width = x_ref.shape[-1]
    rows = x_ref.shape[1]

    @pl.when(pl.program_id(0) == 0)
    def _():
        assemble_triple(triple_ref, triple_full, width)
        assemble_merge(merge_ref, merge_full)

    x = x_ref[0].astype(F32)
    unit, _ = unit_norm(x)
    normed = (unit * vec_ref[0:1] + vec_ref[1:2]).astype(BF16)
    qkv_ref[0, :, 0:width] = (dot(normed, triple_full[:, 0:width]) + vec_ref[3:4]).astype(BF16)
    qkv_ref[0, :, width : 2 * width] = dot(normed, triple_full[:, width : 2 * width]).astype(BF16)
    qkv_ref[0, :, 2 * width : 3 * width] = (
        dot(normed, triple_full[:, 2 * width : 3 * width]) + vec_ref[4:5]
    ).astype(BF16)
    pair = 2 * HEAD_DIM
    first = lax.broadcasted_iota(jnp.int32, (rows, pair), 1) < HEAD_DIM
    live = lax.broadcasted_iota(jnp.int32, (rows, rows), 1) < seq
    scale = HEAD_DIM**-0.5
    zero = jnp.zeros((rows, pair), BF16)
    for p in range(width // pair):
        q = qkv_ref[0, :, p * pair : (p + 1) * pair]
        k = qkv_ref[0, :, width + p * pair : width + (p + 1) * pair]
        v = qkv_ref[0, :, 2 * width + p * pair : 2 * width + (p + 1) * pair]
        outs = []
        for h in range(2):
            mine = first if h == 0 else jnp.logical_not(first)
            logits = dot_rows(jnp.where(mine, q, zero), k) * scale
            logits = jnp.where(live, logits, -1e30)
            top = jnp.max(logits, axis=-1, keepdims=True)
            powers = jnp.exp(logits - top)
            probs = powers * (1.0 / jnp.sum(powers, axis=-1, keepdims=True))
            outs.append(dot(probs.astype(BF16), v))
        attended_ref[0, :, p * pair : (p + 1) * pair] = jnp.where(first, outs[0], outs[1]).astype(BF16)
    middle_ref[0] = x + dot(attended_ref[0], merge_full[...]) + vec_ref[2:3]


def mlp_kernel(
    middle_ref, g_ref, expand_ref, bias_ref, shrink_ref, vec_ref,
    out_ref, dmid_ref, dexpand_ref, dbias_ref, dshrink_ref, sums_ref,
    normed_ref, acc_ref, back_ref,
):
    step = pl.program_id(0)

    @pl.when(step == 0)
    def _():
        unit, _ = unit_norm(middle_ref[...])
        normed_ref[...] = (unit * vec_ref[0:1] + vec_ref[1:2]).astype(BF16)
        acc_ref[...] = jnp.zeros_like(acc_ref)
        back_ref[...] = jnp.zeros_like(back_ref)

    row_count, _, depth, chunk = expand_ref.shape
    expand = expand_ref[...].reshape(row_count * depth, chunk)
    shrink = jnp.concatenate([shrink_ref[r, 0] for r in range(row_count)], axis=-1)
    normed = normed_ref[...]
    g = g_ref[...]
    hidden = dot(normed, expand) + bias_ref[...]
    cdf = 0.5 * (1.0 + lax.erf(hidden * (0.5**0.5)))
    slope = cdf + hidden * (jnp.exp(-0.5 * hidden * hidden) * (1.0 / math.sqrt(2.0 * math.pi)))
    active = (hidden * cdf).astype(BF16)
    acc_ref[...] += dot(active, shrink)
    dhidden_wide = dot_rows(g, shrink) * slope
    dhidden = dhidden_wide.astype(BF16)
    dbias_ref[...] = column_sum(dhidden.astype(F32))
    back_ref[...] += dot_rows(dhidden, expand)
    dshrink = dot_tokens(active, g).astype(BF16)
    cols = dshrink.shape[1] // row_count
    for r in range(row_count):
        dshrink_ref[r, 0] = dshrink[:, r * cols : (r + 1) * cols]
    dexpand_ref[...] = dot_tokens(normed, dhidden).astype(BF16).reshape(row_count, 1, depth, chunk)

    @pl.when(step == pl.num_programs(0) - 1)
    def _():
        middle = middle_ref[...]
        out_ref[...] = (middle + acc_ref[...] + vec_ref[2:3]).astype(BF16)
        unit, inverse = unit_norm(middle)
        wide = g_ref[...].astype(F32)
        back = back_ref[...]
        dmid = wide + norm_backward(back, unit, inverse, vec_ref[0:1])
        dmid_ref[...] = dmid
        sums_ref[0:1] = column_sum(back * unit)
        sums_ref[1:2] = column_sum(back)
        sums_ref[2:3] = column_sum(dmid)
        sums_ref[3:4] = column_sum(wide)


def back_kernel(
    seq, x_ref, dmid_ref, attended_ref, qkv_ref, triple_ref, merge_ref, vec_ref,
    dx_ref, dtriple_ref, dmerge_ref, sums_ref,
    triple_full, merge_full, dqkv_ref, normed_ref, g1_ref, datt_ref,
):
    images, rows, width = x_ref.shape
    assemble_triple(triple_ref, triple_full, width)
    assemble_merge(merge_ref, merge_full)
    pair = 2 * HEAD_DIM
    scale = HEAD_DIM**-0.5
    sums_ref[...] = jnp.zeros_like(sums_ref)

    @pl.loop(0, images)
    def _(image):
        at = pl.ds(pl.multiple_of(image * rows, 16), rows)
        x = x_ref[image].astype(F32)
        unit, inverse = unit_norm(x)
        normed_ref[at, :] = (unit * vec_ref[0:1] + vec_ref[1:2]).astype(BF16)
        dmid = dmid_ref[image]
        g1 = dmid.astype(BF16)
        g1_ref[at, :] = g1
        datt_ref[...] = dot_rows(g1, merge_full[...]).astype(BF16)
        first = lax.broadcasted_iota(jnp.int32, (rows, pair), 1) < HEAD_DIM
        live = lax.broadcasted_iota(jnp.int32, (rows, rows), 0) < seq
        zero = jnp.zeros((rows, pair), BF16)
        for p in range(width // pair):
            q = qkv_ref[image, :, p * pair : (p + 1) * pair]
            k = qkv_ref[image, :, width + p * pair : width + (p + 1) * pair]
            v = qkv_ref[image, :, 2 * width + p * pair : 2 * width + (p + 1) * pair]
            da = datt_ref[:, p * pair : (p + 1) * pair]
            dq, dk, dv = [], [], []
            for h in range(2):
                mine = first if h == 0 else jnp.logical_not(first)
                logits = dot_rows(k, jnp.where(mine, q, zero)) * scale
                logits = jnp.where(live, logits, -1e30)
                top = jnp.max(logits, axis=0, keepdims=True)
                powers = jnp.exp(logits - top)
                probs = powers * (1.0 / column_sum(powers))
                dprobs = dot_rows(v, jnp.where(mine, da, zero))
                weighted = probs * dprobs
                dlogits = ((weighted - probs * column_sum(weighted)) * scale).astype(BF16)
                dq.append(dot_tokens(dlogits, k))
                dk.append(dot(dlogits, q))
                dv.append(dot(probs.astype(BF16), da))
            for t, parts in enumerate((dq, dk, dv)):
                dqkv_ref[at, t * width + p * pair : t * width + (p + 1) * pair] = jnp.where(
                    first, parts[0], parts[1]
                ).astype(BF16)
        dnormed = dot_rows(dqkv_ref[at, :], triple_full[...])
        dx_ref[image] = dmid + norm_backward(dnormed, unit, inverse, vec_ref[0:1])
        sums_ref[0:1] += column_sum(dnormed * unit)
        sums_ref[1:2] += column_sum(dnormed)
        sums_ref[2:3] += column_sum(dqkv_ref[at, 0:width].astype(F32))
        sums_ref[3:4] += column_sum(dqkv_ref[at, 2 * width : 3 * width].astype(F32))

    row_count, col_count, _, depth, cols = dtriple_ref.shape
    for c in range(col_count):

        @pl.loop(0, 3)
        def _(t):
            at = pl.ds(pl.multiple_of(t * width + c * cols, 128), cols)
            part = dot_tokens(normed_ref[...], dqkv_ref[:, at]).astype(BF16)
            for r in range(row_count):
                dtriple_ref[r, c, t] = part[r * depth : (r + 1) * depth]

    attended = attended_ref[...].reshape(images * rows, width)
    for r in range(row_count):
        part = dot_tokens(attended, g1_ref[:, r * cols : (r + 1) * cols]).astype(BF16)
        for c in range(col_count):
            dmerge_ref[r, c] = part[c * depth : (c + 1) * depth]


def whole(shape):
    return pl.BlockSpec(shape, lambda *_: (0,) * len(shape))


def per_image(shape):
    return pl.BlockSpec((1,) + shape, lambda i: (i, 0, 0))


def params():
    return pltpu.CompilerParams(vmem_limit_bytes=VMEM_BYTES)


def attend(x, triple, merge, vec, seq):
    images, rows, width = x.shape
    return pl.pallas_call(
        functools.partial(attend_kernel, seq),
        grid=(images,),
        in_specs=[per_image((rows, width)), whole(triple.shape), whole(merge.shape), whole(vec.shape)],
        out_specs=[per_image((rows, 3 * width)), per_image((rows, width)), per_image((rows, width))],
        out_shape=[
            jax.ShapeDtypeStruct((images, rows, 3 * width), BF16),
            jax.ShapeDtypeStruct((images, rows, width), BF16),
            jax.ShapeDtypeStruct((images, rows, width), F32),
        ],
        scratch_shapes=[pltpu.VMEM((width, 3 * width), BF16), pltpu.VMEM((width, width), BF16)],
        compiler_params=params(),
        name="attend",
    )(x, triple, merge, vec)


def mlp(middle, g, expand, bias, shrink, vec, chunk):
    tokens, width = middle.shape
    row_count, col_count, depth, units = expand.shape
    per_col = units // chunk
    expand_spec = pl.BlockSpec((row_count, 1, depth, chunk), lambda j: (0, j // per_col, 0, j % per_col))
    shrink_spec = pl.BlockSpec((row_count, 1, chunk, depth), lambda j: (0, j // per_col, j % per_col, 0))
    bias_spec = pl.BlockSpec((1, chunk), lambda j: (0, j))
    return pl.pallas_call(
        mlp_kernel,
        grid=(col_count * per_col,),
        in_specs=[whole(middle.shape), whole(g.shape), expand_spec, bias_spec, shrink_spec, whole(vec.shape)],
        out_specs=[whole(middle.shape), whole(middle.shape), expand_spec, bias_spec, shrink_spec, whole((8, width))],
        out_shape=[
            jax.ShapeDtypeStruct((tokens, width), BF16),
            jax.ShapeDtypeStruct((tokens, width), F32),
            jax.ShapeDtypeStruct(expand.shape, BF16),
            jax.ShapeDtypeStruct(bias.shape, F32),
            jax.ShapeDtypeStruct(shrink.shape, BF16),
            jax.ShapeDtypeStruct((8, width), F32),
        ],
        scratch_shapes=[
            pltpu.VMEM((tokens, width), BF16),
            pltpu.VMEM((tokens, width), F32),
            pltpu.VMEM((tokens, width), F32),
        ],
        compiler_params=params(),
        name="mlp",
    )(middle, g, expand, bias, shrink, vec)


def attend_back(x, dmid, attended, qkv, triple, merge, vec, seq):
    images, rows, width = x.shape
    return pl.pallas_call(
        functools.partial(back_kernel, seq),
        out_shape=[
            jax.ShapeDtypeStruct((images, rows, width), F32),
            jax.ShapeDtypeStruct(triple.shape, BF16),
            jax.ShapeDtypeStruct(merge.shape, BF16),
            jax.ShapeDtypeStruct((8, width), F32),
        ],
        scratch_shapes=[
            pltpu.VMEM((width, 3 * width), BF16),
            pltpu.VMEM((width, width), BF16),
            pltpu.VMEM((images * rows, 3 * width), BF16),
            pltpu.VMEM((images * rows, width), BF16),
            pltpu.VMEM((images * rows, width), BF16),
            pltpu.VMEM((rows, width), BF16),
        ],
        compiler_params=params(),
        name="attend_back",
    )(x, dmid, attended, qkv, triple, merge, vec)


def gather_blocks(block, row_count, col_count):
    half = lax.all_gather(block, "col", axis=0, tiled=False)
    return lax.all_gather(half, "row", axis=0, tiled=False)


def owned_total(blocks):
    mine = lax.psum_scatter(blocks, "row", scatter_dimension=0, tiled=False)
    mine = lax.psum_scatter(mine, "col", scatter_dimension=0, tiled=False)
    return lax.psum(mine, "dp").astype(F32)


def on_device(
    tokens,
    cotangent,
    triple_weight,
    attend_bias,
    merge_weight,
    expand_weight,
    expand_bias,
    shrink_weight,
    norm_gain,
    norm_shift,
    branch_bias,
):
    row_count, col_count = lax.axis_size("row"), lax.axis_size("col")
    images, seq, width = tokens.shape
    rows = -(-seq // 16) * 16
    pad = ((0, 0), (0, rows - seq), (0, 0))
    x = jnp.pad(tokens, pad)
    g = jnp.pad(cotangent, pad).reshape(images * rows, width)
    biases = jnp.concatenate([attend_bias[0], attend_bias[1], expand_bias])
    biases = lax.all_gather(biases, "col", axis=0, tiled=False)
    local = attend_bias.shape[1]
    attend_full = [biases[:, t * local : (t + 1) * local].reshape(1, width) for t in range(2)]
    hidden_bias = biases[:, 2 * local :].reshape(1, -1)
    triple = gather_blocks(triple_weight.transpose(1, 0, 2), row_count, col_count)
    merge = gather_blocks(merge_weight, row_count, col_count)
    expand = gather_blocks(expand_weight, row_count, col_count)
    shrink = gather_blocks(shrink_weight, row_count, col_count)
    filler = jnp.zeros((3, width), F32)
    vec_one = jnp.concatenate([norm_gain[0:1], norm_shift[0:1], branch_bias[0:1]] + attend_full + [filler])
    vec_two = jnp.concatenate([norm_gain[1:2], norm_shift[1:2], branch_bias[1:2], filler, filler[:2]])
    qkv, attended, middle = attend(x, triple, merge, vec_one, seq)
    out, dmid, dexpand, dbias, dshrink, sums_two = mlp(
        middle.reshape(images * rows, width), g, expand, hidden_bias, shrink, vec_two, expand_weight.shape[1] // 3
    )
    dx, dtriple, dmerge, sums_one = attend_back(
        x, dmid.reshape(images, rows, width), attended, qkv, triple, merge, vec_one, seq
    )
    shared = jnp.concatenate([sums_one[0:4], sums_two[0:4], dbias.reshape(-1, width)])
    shared = lax.psum(shared, ("dp", "row", "col"))
    col_at = lax.axis_index("col")
    units = expand_bias.shape[0]
    attend_grad = lax.dynamic_slice_in_dim(shared[2:4], col_at * local, local, 1)
    hidden_grad = lax.dynamic_slice_in_dim(shared[8:].reshape(-1), col_at * units, units, 0)
    return (
        out.reshape(images, rows, width)[:, :seq],
        dx[:, :seq],
        owned_total(dtriple).transpose(1, 0, 2),
        attend_grad,
        owned_total(dmerge),
        owned_total(dexpand),
        hidden_grad,
        owned_total(dshrink),
        jnp.stack([shared[0], shared[4]]),
        jnp.stack([shared[1], shared[5]]),
        shared[6:8],
    )


def solution(mesh):
    placed = (
        P(("dp", "row", "col"), None, None),
        P(("dp", "row", "col"), None, None),
        P("row", None, "col"),
        P(None, "col"),
        P("col", "row"),
        P("row", "col"),
        P("col"),
        P("col", "row"),
        P(),
        P(),
        P(),
    )
    return jax.shard_map(
        on_device,
        mesh=mesh,
        in_specs=placed,
        out_specs=(
            P(("dp", "row", "col"), None, None),
            P(("dp", "row", "col"), None, None),
            P("row", None, "col"),
            P(None, "col"),
            P("col", "row"),
            P("row", "col"),
            P("col"),
            P("col", "row"),
            P(),
            P(),
            P(),
        ),
        check_vma=False,
    )
```

time: 875 us -> 594 us (0.68); the launches traced: 865 us -> 594 us
  matrix products: 148 us -> 0 us
  Pallas kernels: 0 us -> 93.8 us
  waiting for transfers between devices: 495 us -> 406 us
  blocking collectives: 105 us -> 58.8 us
  other arithmetic: 50.4 us -> 8.7 us
  local copies, waits for them, and re-layouts: 50 us -> 11.8 us
    dot_general x18 -> x0, matrix products: 148 us -> none  [the longest x1 19.1 us: on_device(): jnp.einsum('nhqk,nkhe->nqhe', grad_logits, to_heads(key_rows), preferred_...]
    psum x1, waiting for transfers between devices: 190 us -> 92.3 us  [owned_total(): return lax.psum(mine, 'dp').astype(F32)]
    pallas_call x0 -> x3, Pallas kernels: none -> 93.8 us  [the longest x1 40.4 us: attend_back(): pl.pallas_call(functools.partial(back_kernel, seq), out_shape=[jax.ShapeD...]
    psum x1 -> x0, blocking collectives: 61.9 us -> none  [on_device(): lax.psum((attend_part, hidden_part), ('dp', 'row'))]
    convert_element_type x4 -> x3, other arithmetic: 29.6 us -> 5.47 us  [owned_total(): return lax.psum(mine, 'dp').astype(F32)]
    unnamed x69 -> x43, local copies, waits for them, and re-layouts: 27.2 us -> 5.52 us
    reduce_sum x7 -> x0, other arithmetic: 18.4 us -> none  [the longest x1 4.31 us: on_device(): jnp.sum(grad_middle, axis=(0, 1))]
    slice x10 -> x11, local copies, waits for them, and re-layouts: 13.8 us -> 0.93 us  [the longest x1 0.6 us: on_device(): shared[6:8]]
  transfers between devices with their start and end apart: 16 -> 16, of which waited for: 11 -> 16; matrix products, arithmetic and copies ran while one was open for 20% -> 2% of each run, Pallas kernels for 0% -> 3%
where the time goes in v1:
time: 594 us
  waiting for transfers between devices  406 us (68%)
  Pallas kernels  93.8 us (16%)
  blocking collectives  58.8 us (10%)
  between operations  14.3 us (2%)
  local copies, waits for them, and re-layouts  11.8 us (2%)
  other arithmetic  8.7 us (1%)
    reduce_scatter x4, waiting for transfers between devices, owned_total(): mine = lax.psum_scatter(mine, 'col', scatter_dimension=0, tiled=False)  123 us
    all_gather x3, waiting for transfers between devices, gather_blocks(): half = lax.all_gather(block, 'col', axis=0, tiled=False)  96.6 us
    psum x1, waiting for transfers between devices, owned_total(): return lax.psum(mine, 'dp').astype(F32)  92.3 us
    reduce_scatter x4, waiting for transfers between devices, owned_total(): mine = lax.psum_scatter(blocks, 'row', scatter_dimension=0, tiled=False)  54.8 us
    psum x1, blocking collectives, on_device(): shared = lax.psum(shared, ('dp', 'row', 'col'))  43.6 us
    pallas_call x1, Pallas kernels, attend_back(): pl.pallas_call(functools.partial(back_kernel, seq), out_shape=[jax.ShapeD...  40.4 us
    pallas_call x1, Pallas kernels, mlp(): pl.pallas_call(mlp_kernel, grid=(col_count * per_col,), in_specs=[whole(m...  37.4 us
    all_gather x4, waiting for transfers between devices, gather_blocks(): return lax.all_gather(half, 'row', axis=0, tiled=False)  34.9 us
  transfers between devices with their start and end apart: 16, of which 16 were waited for; matrix products, arithmetic and copies ran while one was open for 2% of the time, Pallas kernels for 3%

profile of v1, /device:TPU:0, one launch (start us, length us, event | category | flops | bytes accessed | tf_op | source)
XLA Modules:
  0.0 593.6 jit_solution(2643255978140391242)
XLA Ops:
  7.2 0.7 all-gather.18.cloned.1.call-update
  8.0 0.7 all-gather.28.cloned.1.call-update
  8.7 0.7 all-gather.24.cloned.1.call-update
  9.5 10.7 %all-gather.2 = bf16[768,384]{1,0:T(8,128)(2,1)} all-gather(bf16[384,384]{1,0:T(8,128)(2,1)S(1)} %copy-done.6), channel_id=4, replica_groups=mesh['dp'=8,'row'=2,'col'=2] {'col'}, dimensions={0}, use_global_device_ids=true | all-gather | bytes 884736 | tf_op jit(solution)/shard_map/all_gather | solution.py:311
  20.3 21.5 %all-gather.18.cloned.1.call-done = bf16[6,384,384]{2,1,0:T(8,128)(2,1)} async-done(((bf16[3,384,384]{2,1,0:T(8,128)(2,1)}), bf16[6,384,384]{2,1,0:T(8,128)(2,1)}) %all-gather.18.cloned.1.call-update) | async-done | bytes 1769488 | tf_op jit(solution)/shard_map/all_gather | solution.py:311
  41.8 37.6 %all-gather.28.cloned.1.call-done = bf16[3072,384]{1,0:T(8,128)(2,1)} async-done(((bf16[1536,384]{1,0:T(8,128)(2,1)}), bf16[3072,384]{1,0:T(8,128)(2,1)}) %all-gather.28.cloned.1.call-update) | async-done | bytes 2359312 | tf_op jit(solution)/shard_map/all_gather | solution.py:311
  79.5 37.5 %all-gather.24.cloned.1.call-done = bf16[768,1536]{1,0:T(8,128)(2,1)} async-done(((bf16[384,1536]{1,0:T(8,128)(2,1)}), bf16[768,1536]{1,0:T(8,128)(2,1)}) %all-gather.24.cloned.1.call-update) | async-done | bytes 2359312 | tf_op jit(solution)/shard_map/all_gather | solution.py:311
  117.2 4.5 all-gather.9
  121.9 0.6 copy.35
  122.6 1.1 pad.7.x_ref
  123.8 1.1 pad.8.clone
  125.0 0.6 concatenate.14.vec_ref
  125.6 0.6 concatenate.13.vec_ref
  126.3 1.4 all-gather.22.cloned.1.call-done
  127.7 15.3 %all-gather.20.cloned.1.call-done = bf16[4,3,384,384]{3,2,1,0:T(8,128)(2,1)} async-done(((bf16[2,3,384,384]{3,2,1,0:T(8,128)(2,1)}), bf16[4,3,384,384]{3,2,1,0:T(8,128)(2,1)}) %all-gather.20.cloned.1.call-update) | async-done | bytes 3538960 | tf_op jit(solution)/shard_map/all_gather | solution.py:312
  143.0 16.0 %attend.1 = (bf16[4,208,2304]{2,1,0:T(8,128)(2,1)}, bf16[4,208,768]{2,1,0:T(8,128)(2,1)}, f32[4,208,768]{2,1,0:T(8,128)}) custom-call(bf16[4,208,768]{2,1,0:T(8,128)(2,1)} %pad.7.x_ref, bf16[2,2,3,384,384]{4,3,2,1,0:T(8,128)(2,1)} %bitcast.38, bf16[2,2,384,384]{3,2,1,0:T(8,128)(2,1)} %bitcast.41, f32[8,768]{1,0:T(8,128)} %concatenate.13.vec_ref), custom_call_target="tpu_custom_call" | custom-call | tf_op jit(solution)/shard_map/attend/pallas_call | solution.py:241
  159.0 1.0 all-gather.30.cloned.1.call-done
  160.0 17.2 %all-gather.26.cloned.1.call-done = bf16[4,384,1536]{2,1,0:T(8,128)(2,1)} async-done(((bf16[2,384,1536]{2,1,0:T(8,128)(2,1)}), bf16[4,384,1536]{2,1,0:T(8,128)(2,1)}) %all-gather.26.cloned.1.call-update) | async-done | bytes 4718608 | tf_op jit(solution)/shard_map/all_gather | solution.py:312
  177.2 37.4 %mlp.1 = (bf16[832,768]{1,0:T(8,128)(2,1)}, f32[832,768]{1,0:T(8,128)}, bf16[2,2,384,1536]{3,2,1,0:T(8,128)(2,1)}, f32[1,3072]{1,0:T(1,128)}, bf16[2,2,1536,384]{3,2,1,0:T(8,128)(2,1)}, /*index=5*/f32[8,768]{1,0:T(8,128)}) custom-call(f32[832,768]{1,0:T(8,128)} %bitcast.46, bf16[832,768]{1,0:T(8,128)(2,1)} %bitcast.40, bf16[2,2,384,1536]{3,2,1,0:T(8,128)(2,1)} %bitcast.44, ...), custom_call_target="tpu_custom_call" | custom-call | tf_op jit(solution)/shard_map/mlp/pallas_call | solution.py:264
  214.6 40.4 %attend_back.1 = (f32[4,208,768]{2,1,0:T(8,128)}, bf16[2,2,3,384,384]{4,3,2,1,0:T(8,128)(2,1)}, bf16[2,2,384,384]{3,2,1,0:T(8,128)(2,1)}, f32[8,768]{1,0:T(8,128)}) custom-call(bf16[4,208,768]{2,1,0:T(8,128)(2,1)} %pad.7.x_ref, f32[4,208,768]{2,1,0:T(8,128)} %bitcast.45, bf16[4,208,768]{2,1,0:T(8,128)(2,1)} %get-tuple-element.27.attended_ref, ...), custom_call_target="tpu_custom_call" | custom-call | tf_op jit(solution)/shard_map/attend_back/pallas_call | solution.py:289
  255.1 0.7 reduce-scatter.9.cloned.1.call-update
  255.8 0.5 reduce-scatter.17.cloned.1.call-update
  256.4 0.7 reduce-scatter.21.cloned.1.call-update
  257.1 7.9 %reduce-scatter.13.cloned.1.call-done = bf16[1,2,384,384]{3,2,1,0:T(8,128)(2,1)} async-done(((bf16[2,2,384,384]{3,2,1,0:T(8,128)(2,1)}), bf16[1,2,384,384]{3,2,1,0:T(8,128)(2,1)}) %reduce-scatter.13.cloned.1.call-update) | async-done | bytes 589840 | tf_op jit(solution)/shard_map/reduce_scatter | solution.py:316
  265.1 14.9 %reduce-scatter.9.cloned.1.call-done = bf16[1,2,3,384,384]{4,3,2,1,0:T(8,128)(2,1)} async-done(((bf16[2,2,3,384,384]{4,3,2,1,0:T(8,128)(2,1)}), bf16[1,2,3,384,384]{4,3,2,1,0:T(8,128)(2,1)}) %reduce-scatter.9.cloned.1.call-update) | async-done | bytes 1769488 | tf_op jit(solution)/shard_map/reduce_scatter | solution.py:316
  280.0 15.9 %reduce-scatter.17.cloned.1.call-done = bf16[1,2,384,1536]{3,2,1,0:T(8,128)(2,1)} async-done(((bf16[2,2,384,1536]{3,2,1,0:T(8,128)(2,1)}), bf16[1,2,384,1536]{3,2,1,0:T(8,128)(2,1)}) %reduce-scatter.17.cloned.1.call-update) | async-done | bytes 2359312 | tf_op jit(solution)/shard_map/reduce_scatter | solution.py:316
  296.0 16.1 %reduce-scatter.21.cloned.1.call-done = bf16[1,2,1536,384]{3,2,1,0:T(8,128)(2,1)} async-done(((bf16[2,2,1536,384]{3,2,1,0:T(8,128)(2,1)}), bf16[1,2,1536,384]{3,2,1,0:T(8,128)(2,1)}) %reduce-scatter.21.cloned.1.call-update) | async-done | bytes 2359312 | tf_op jit(solution)/shard_map/reduce_scatter | solution.py:316
  312.2 18.5 %reduce-scatter.15.cloned.1.call-done = bf16[1,384,384]{2,1,0:T(8,128)(2,1)} async-done(((bf16[2,384,384]{2,1,0:T(8,128)(2,1)}), bf16[1,384,384]{2,1,0:T(8,128)(2,1)}) %reduce-scatter.15.cloned.1.call-update) | async-done | bytes 294928 | tf_op jit(solution)/shard_map/reduce_scatter | solution.py:317
  330.7 30.6 %reduce-scatter.11.cloned.1.call-done = bf16[1,3,384,384]{3,2,1,0:T(8,128)(2,1)} async-done(((bf16[2,3,384,384]{3,2,1,0:T(8,128)(2,1)}), bf16[1,3,384,384]{3,2,1,0:T(8,128)(2,1)}) %reduce-scatter.11.cloned.1.call-update) | async-done | bytes 884752 | tf_op jit(solution)/shard_map/reduce_scatter | solution.py:317
  361.3 36.8 %reduce-scatter.19.cloned.1.call-done = bf16[1,384,1536]{2,1,0:T(8,128)(2,1)} async-done(((bf16[2,384,1536]{2,1,0:T(8,128)(2,1)}), bf16[1,384,1536]{2,1,0:T(8,128)(2,1)}) %reduce-scatter.19.cloned.1.call-update) | async-done | bytes 1179664 | tf_op jit(solution)/shard_map/reduce_scatter | solution.py:317
  398.2 36.9 %reduce-scatter.23.cloned.1.call-done = bf16[1,1536,384]{2,1,0:T(8,128)(2,1)} async-done(((bf16[2,1536,384]{2,1,0:T(8,128)(2,1)}), bf16[1,1536,384]{2,1,0:T(8,128)(2,1)}) %reduce-scatter.23.cloned.1.call-update) | async-done | bytes 1179664 | tf_op jit(solution)/shard_map/reduce_scatter | solution.py:317
  435.1 0.7 copy-done.11
  435.8 0.5 broadcast.9
  436.3 0.7 reduce.7
  437.1 43.6 %psum.36 = f32[12,768]{1,0:T(8,128)S(1)} all-reduce(f32[12,768]{1,0:T(8,128)S(1)} %pad_maximum_fusion), channel_id=1, replica_groups=mesh['dp'=8,'row'=2,'col'=2] {'dp','row','col'}, use_global_device_ids=true, to_apply=%region_3.4 | all-reduce | flops 9216 | bytes 73728 | tf_op jit(solution)/shard_map/psum | solution.py:360
  480.7 0.2 slice.82
  480.9 2.4 copy.29
  483.4 1.5 copy.31
  484.9 0.7 dynamic_slice.7
  485.5 0.6 fusion
  486.1 0.6 constant_dynamic-slice_fusion
  486.7 0.6 pad_maximum_fusion.3
  487.3 0.6 pad_maximum_fusion.2
  487.9 92.3 %all-reduce.5.cloned.1.call-done = (bf16[384,3,384]{2,0,1:T(8,128)(2,1)}, bf16[384,384]{1,0:T(8,128)(2,1)}, bf16[384,1536]{1,0:T(8,128)(2,1)}, bf16[1536,384]{1,0:T(8,128)(2,1)}) async-done(((bf16[384,3,384]{2,0,1:T(8,128)(2,1)}, bf16[384,384]{1,0:T(8,128)(2,1)}, bf16[384,1536]{1,0:T(8,128)(2,1)}, bf16[1536,384]{1,0:T(8,128)(2,1)}), (bf16[384,3,384]{2,0,1:T(8,128)(2,1)}, bf16[384,384]{1,0:T(8,128)(2,1)}, ...) | async-done | bytes 3538960 | tf_op jit(solution)/shard_map/psum | solution.py:318
  580.3 3.1 convert_element_type.14
  583.3 1.6 convert_element_type.15
  584.9 1.3 transpose.11
  586.2 0.9 convert_element_type.13
  (79 shorter events, 1.3 us)
Async XLA Ops:
  7.2 2.3 copy-start.6
  7.2 34.5 %all-gather.18.cloned.1.call-start = ((), (), s32[]{:S(2)}) async-start(), calls=%async_computation.16 | async-start | bytes 2654208 | tf_op jit(solution)/shard_map/all_gather | solution.py:311
  7.9 71.5 %all-gather.28.cloned.1.call-start = ((), (), s32[]{:S(2)}) async-start(), calls=%async_computation.21 | async-start | bytes 3538944 | tf_op jit(solution)/shard_map/all_gather | solution.py:311
  8.7 108.4 %all-gather.24.cloned.1.call-start = ((), (), s32[]{:S(2)}) async-start(), calls=%async_computation.19 | async-start | bytes 3538944 | tf_op jit(solution)/shard_map/all_gather | solution.py:311
  9.4 118.3 %all-gather.22.cloned.1.call-start = ((), (), s32[]{:S(2)}) async-start(), calls=%async_computation.18 | async-start | bytes 1769472 | tf_op jit(solution)/shard_map/all_gather | solution.py:312
  20.2 122.8 %all-gather.20.cloned.1.call-start = ((), (), s32[]{:S(2)}) async-start(), calls=%async_computation.17 | async-start | bytes 5308416 | tf_op jit(solution)/shard_map/all_gather | solution.py:312
  41.8 118.3 %all-gather.30.cloned.1.call-start = ((), (), s32[]{:S(2)}) async-start(), calls=%async_computation.22 | async-start | bytes 7077888 | tf_op jit(solution)/shard_map/all_gather | solution.py:312
  79.4 37.7 %copy-start.15 = (f32[2,384]{1,0:T(2,128)S(1)}, f32[2,384]{1,0:T(2,128)}, u32[]{:S(2)}) copy-start(f32[2,384]{1,0:T(2,128)} %param.14) | copy-start | bytes 9220
  79.4 37.7 %copy-start.9 = (f32[1536]{0:T(1024)S(1)}, f32[1536]{0:T(1024)}, u32[]{:S(2)}) copy-start(f32[1536]{0:T(1024)} %param.17) | copy-start | bytes 18436
  79.4 42.3 %copy-start.1 = (bf16[4,197,768]{2,0,1:T(4,128)(2,1)S(1)}, bf16[4,197,768]{2,0,1:T(4,128)(2,1)}, u32[]{:S(2)}) copy-start(bf16[4,197,768]{2,0,1:T(4,128)(2,1)} %param.11) | copy-start | bytes 3631108
  79.4 97.8 %all-gather.26.cloned.1.call-start = ((), (), s32[]{:S(2)}) async-start(), calls=%async_computation.20 | async-start | bytes 7077888 | tf_op jit(solution)/shard_map/all_gather | solution.py:312
  117.1 5.5 copy-start.2
  117.1 147.9 %reduce-scatter.13.cloned.1.call-start = ((), (), s32[]{:S(2)}) async-start(), calls=%async_computation.10 | async-start | bytes 1769472 | tf_op jit(solution)/shard_map/reduce_scatter | solution.py:316
  123.8 1.1 copy-start.12
  123.8 1.1 copy-start.13
  123.8 1.2 copy-start.14
  255.0 24.9 %reduce-scatter.9.cloned.1.call-start = ((), (), s32[]{:S(2)}) async-start(), calls=%async_computation.8 | async-start | bytes 5308416 | tf_op jit(solution)/shard_map/reduce_scatter | solution.py:316
  255.7 40.2 %reduce-scatter.17.cloned.1.call-start = ((), (), s32[]{:S(2)}) async-start(), calls=%async_computation.12 | async-start | bytes 7077888 | tf_op jit(solution)/shard_map/reduce_scatter | solution.py:316
  256.3 55.8 %reduce-scatter.21.cloned.1.call-start = ((), (), s32[]{:S(2)}) async-start(), calls=%async_computation.14 | async-start | bytes 7077888 | tf_op jit(solution)/shard_map/reduce_scatter | solution.py:316
  257.1 73.7 %reduce-scatter.15.cloned.1.call-start = ((), (), s32[]{:S(2)}) async-start(), calls=%async_computation.11 | async-start | bytes 884736 | tf_op jit(solution)/shard_map/reduce_scatter | solution.py:317
  265.0 96.3 %reduce-scatter.11.cloned.1.call-start = ((), (), s32[]{:S(2)}) async-start(), calls=%async_computation.9 | async-start | bytes 2654208 | tf_op jit(solution)/shard_map/reduce_scatter | solution.py:317
  280.0 118.2 %reduce-scatter.19.cloned.1.call-start = ((), (), s32[]{:S(2)}) async-start(), calls=%async_computation.13 | async-start | bytes 3538944 | tf_op jit(solution)/shard_map/reduce_scatter | solution.py:317
  295.9 139.1 %reduce-scatter.23.cloned.1.call-start = ((), (), s32[]{:S(2)}) async-start(), calls=%async_computation.15 | async-start | bytes 3538944 | tf_op jit(solution)/shard_map/reduce_scatter | solution.py:317
  312.2 268.1 %all-reduce.5.cloned.1.call-start = ((), (), s32[]{:S(2)}) async-start(), calls=%async_computation.23 | async-start | bytes 7077888 | tf_op jit(solution)/shard_map/psum | solution.py:318
  435.1 0.7 copy-start.11
  435.1 1.3 copy-start.8
  435.1 1.9 copy-start.10
  435.1 45.6 %copy-start = (f32[4,208,768]{2,1,0:T(8,128)S(1)}, f32[4,208,768]{2,1,0:T(8,128)}, u32[]{:S(2)}) copy-start(f32[4,208,768]{2,1,0:T(8,128)} %get-tuple-element.29) | copy-start | bytes 7667716
  480.9 2.4 copy-start.3
  580.3 3.1 copy-start.4
  583.3 1.6 copy-start.5
  584.9 1.3 copy-start.7
Sparse Core Ops, SparseCore 0:
  9.6 32.1 all-gather.17
  43.3 36.0 all-gather.27
  80.9 36.0 all-gather.23
  118.4 9.2 all-gather.21
  129.1 13.8 all-gather.19
  144.4 15.5 all-gather.29
  161.6 15.5 all-gather.25
  255.1 9.8 reduce-scatter.12
  267.3 12.5 reduce-scatter.8
  282.1 13.7 reduce-scatter.16
  298.3 13.7 reduce-scatter.20
  314.2 16.4 reduce-scatter.14
  333.1 28.1 reduce-scatter.10
  363.4 34.7 reduce-scatter.18
  400.3 34.6 reduce-scatter.22
  438.9 141.3 all-reduce.4

commit v2 on v1

v2 whole, which is shorter than its diff:
```python
import functools
import math

import jax
import jax.numpy as jnp
from jax import lax
from jax.experimental import pallas as pl
from jax.experimental.pallas import tpu as pltpu
from jax.sharding import PartitionSpec as P

HEAD_DIM = 64
EPSILON = 1e-06
F32 = jnp.float32
BF16 = jnp.bfloat16
VMEM_BYTES = 56 * 1024 * 1024


def mean_rows(source):
    return jnp.mean(source, axis=-1, keepdims=True)


def unit_norm(source):
    average = mean_rows(source)
    variance = mean_rows(source * source) - average * average
    inverse = lax.rsqrt(variance + EPSILON)
    return (source - average) * inverse, inverse


def norm_backward(grad, unit, inverse, gain):
    scaled = grad * gain
    return inverse * (scaled - mean_rows(scaled) - unit * mean_rows(scaled * unit))


def dot(left, right):
    return jnp.dot(left, right, preferred_element_type=F32)


def dot_rows(left, right):
    return lax.dot_general(left, right, (((1,), (1,)), ((), ())), preferred_element_type=F32)


def dot_tokens(left, right):
    return lax.dot_general(left, right, (((0,), (0,)), ((), ())), preferred_element_type=F32)


def column_sum(source):
    return jnp.sum(source, axis=0, keepdims=True)


def assemble(block_refs, triple_full, merge_full):
    depth = block_refs[0].shape[1]
    width = 2 * depth
    for r in range(2):
        for c in range(2):
            block = block_refs[2 * r + c]
            for t in range(3):
                triple_full[r * depth : (r + 1) * depth, t * width + c * depth : t * width + (c + 1) * depth] = (
                    block[t * depth : (t + 1) * depth]
                )
            merge_full[c * depth : (c + 1) * depth, r * depth : (r + 1) * depth] = block[3 * depth : 4 * depth]


def attend_kernel(seq, x_ref, own, across, twin, twin_across, vec_ref, qkv_ref, attended_ref, middle_ref, triple_full, merge_full):
    width = x_ref.shape[-1]
    rows = x_ref.shape[1]

    @pl.when(pl.program_id(0) == 0)
    def _():
        assemble((own, across, twin, twin_across), triple_full, merge_full)

    x = x_ref[0].astype(F32)
    unit, _ = unit_norm(x)
    normed = (unit * vec_ref[0:1] + vec_ref[1:2]).astype(BF16)
    qkv_ref[0, :, 0:width] = (dot(normed, triple_full[:, 0:width]) + vec_ref[3:4]).astype(BF16)
    qkv_ref[0, :, width : 2 * width] = dot(normed, triple_full[:, width : 2 * width]).astype(BF16)
    qkv_ref[0, :, 2 * width : 3 * width] = (
        dot(normed, triple_full[:, 2 * width : 3 * width]) + vec_ref[4:5]
    ).astype(BF16)
    pair = 2 * HEAD_DIM
    first = lax.broadcasted_iota(jnp.int32, (rows, pair), 1) < HEAD_DIM
    live = lax.broadcasted_iota(jnp.int32, (rows, rows), 1) < seq
    scale = HEAD_DIM**-0.5
    zero = jnp.zeros((rows, pair), BF16)
    for p in range(width // pair):
        q = qkv_ref[0, :, p * pair : (p + 1) * pair]
        k = qkv_ref[0, :, width + p * pair : width + (p + 1) * pair]
        v = qkv_ref[0, :, 2 * width + p * pair : 2 * width + (p + 1) * pair]
        outs = []
        for h in range(2):
            mine = first if h == 0 else jnp.logical_not(first)
            logits = dot_rows(jnp.where(mine, q, zero), k) * scale
            logits = jnp.where(live, logits, -1e30)
            top = jnp.max(logits, axis=-1, keepdims=True)
            powers = jnp.exp(logits - top)
            probs = powers * (1.0 / jnp.sum(powers, axis=-1, keepdims=True))
            outs.append(dot(probs.astype(BF16), v))
        attended_ref[0, :, p * pair : (p + 1) * pair] = jnp.where(first, outs[0], outs[1]).astype(BF16)
    middle_ref[0] = x + dot(attended_ref[0], merge_full[...]) + vec_ref[2:3]


def mlp_kernel(final, middle_ref, g_ref, e0, e1, bias_ref, s0, s1, vec_ref, *refs):
    if final:
        acc_in, back_in, out_ref, dmid_ref, dexpand_ref, dbias_ref, dshrink_ref, sums_ref, normed_ref, acc_ref, back_ref = refs
    else:
        acc_ref, back_ref, dexpand_ref, dbias_ref, dshrink_ref, normed_ref = refs
    step = pl.program_id(0)

    @pl.when(step == 0)
    def _():
        unit, _ = unit_norm(middle_ref[...])
        normed_ref[...] = (unit * vec_ref[0:1] + vec_ref[1:2]).astype(BF16)
        if final:
            acc_ref[...] = acc_in[...]
            back_ref[...] = back_in[...]
        else:
            acc_ref[...] = jnp.zeros_like(acc_ref)
            back_ref[...] = jnp.zeros_like(back_ref)

    expand = jnp.concatenate([e0[...], e1[...]], axis=0)
    shrink = jnp.concatenate([s0[...], s1[...]], axis=1)
    normed = normed_ref[...]
    g = g_ref[...]
    hidden = dot(normed, expand) + bias_ref[...]
    cdf = 0.5 * (1.0 + lax.erf(hidden * (0.5**0.5)))
    slope = cdf + hidden * (jnp.exp(-0.5 * hidden * hidden) * (1.0 / math.sqrt(2.0 * math.pi)))
    active = (hidden * cdf).astype(BF16)
    acc_ref[...] += dot(active, shrink)
    dhidden = (dot_rows(g, shrink) * slope).astype(BF16)
    dbias_ref[...] = column_sum(dhidden.astype(F32))
    back_ref[...] += dot_rows(dhidden, expand)
    dshrink = dot_tokens(active, g).astype(BF16)
    dexpand = dot_tokens(dhidden, normed).astype(BF16)
    cols = dshrink.shape[1] // 2
    for r in range(2):
        dshrink_ref[r] = dshrink[:, r * cols : (r + 1) * cols]
        dexpand_ref[r] = dexpand[:, r * cols : (r + 1) * cols]

    if final:

        @pl.when(step == pl.num_programs(0) - 1)
        def _():
            middle = middle_ref[...]
            out_ref[...] = (middle + acc_ref[...] + vec_ref[2:3]).astype(BF16)
            unit, inverse = unit_norm(middle)
            wide = g_ref[...].astype(F32)
            back = back_ref[...]
            dmid = wide + norm_backward(back, unit, inverse, vec_ref[0:1])
            dmid_ref[...] = dmid
            sums_ref[0:1] = column_sum(back * unit)
            sums_ref[1:2] = column_sum(back)
            sums_ref[2:3] = column_sum(dmid)
            sums_ref[3:4] = column_sum(wide)


def back_kernel(
    seq, x_ref, dmid_ref, qkv_ref, own, across, twin, twin_across, vec_ref,
    dx_ref, dqkv_ref, normed_ref, sums_ref,
    triple_full, merge_full, datt_ref,
):
    images, rows, width = x_ref.shape
    assemble((own, across, twin, twin_across), triple_full, merge_full)
    pair = 2 * HEAD_DIM
    scale = HEAD_DIM**-0.5
    sums_ref[...] = jnp.zeros_like(sums_ref)

    @pl.loop(0, images)
    def _(image):
        x = x_ref[image].astype(F32)
        unit, inverse = unit_norm(x)
        normed_ref[image] = (unit * vec_ref[0:1] + vec_ref[1:2]).astype(BF16)
        dmid = dmid_ref[image]
        g1 = dmid.astype(BF16)
        datt_ref[...] = dot_rows(g1, merge_full[...]).astype(BF16)
        first = lax.broadcasted_iota(jnp.int32, (rows, pair), 1) < HEAD_DIM
        live = lax.broadcasted_iota(jnp.int32, (rows, rows), 0) < seq
        zero = jnp.zeros((rows, pair), BF16)
        for p in range(width // pair):
            q = qkv_ref[image, :, p * pair : (p + 1) * pair]
            k = qkv_ref[image, :, width + p * pair : width + (p + 1) * pair]
            v = qkv_ref[image, :, 2 * width + p * pair : 2 * width + (p + 1) * pair]
            da = datt_ref[:, p * pair : (p + 1) * pair]
            dq, dk, dv = [], [], []
            for h in range(2):
                mine = first if h == 0 else jnp.logical_not(first)
                logits = dot_rows(k, jnp.where(mine, q, zero)) * scale
                logits = jnp.where(live, logits, -1e30)
                top = jnp.max(logits, axis=0, keepdims=True)
                powers = jnp.exp(logits - top)
                probs = powers * (1.0 / column_sum(powers))
                dprobs = dot_rows(v, jnp.where(mine, da, zero))
                weighted = probs * dprobs
                dlogits = ((weighted - probs * column_sum(weighted)) * scale).astype(BF16)
                dq.append(dot_tokens(dlogits, k))
                dk.append(dot(dlogits, q))
                dv.append(dot(probs.astype(BF16), da))
            for t, parts in enumerate((dq, dk, dv)):
                dqkv_ref[image, :, t * width + p * pair : t * width + (p + 1) * pair] = jnp.where(
                    first, parts[0], parts[1]
                ).astype(BF16)
        dnormed = dot_rows(dqkv_ref[image], triple_full[...])
        dx_ref[image] = dmid + norm_backward(dnormed, unit, inverse, vec_ref[0:1])
        sums_ref[0:1] += column_sum(dnormed * unit)
        sums_ref[1:2] += column_sum(dnormed)
        sums_ref[2:3] += column_sum(dqkv_ref[image, :, 0:width].astype(F32))
        sums_ref[3:4] += column_sum(dqkv_ref[image, :, 2 * width : 3 * width].astype(F32))


def weights_kernel(
    count, *refs,
):
    normed_refs, dqkv_refs = refs[:count], refs[count : 2 * count]
    attended_ref, dmid_ref, dfirst_ref, dsecond_ref = refs[2 * count :]
    width = attended_ref.shape[-1]
    depth = cols = width // 2

    def tall(parts):
        return parts.reshape(parts.shape[0] * parts.shape[1], parts.shape[2])

    normed = jnp.concatenate([tall(ref[...]) for ref in normed_refs], axis=0)
    for c in range(2):
        for t in range(3):
            at = t * width + c * cols
            grads = jnp.concatenate([tall(ref[:, :, at : at + cols]) for ref in dqkv_refs], axis=0)
            part = dot_tokens(normed, grads).astype(BF16)
            for r in range(2):
                home = dfirst_ref if t < 2 else dsecond_ref
                home[r, c, t % 2 * depth : (t % 2 + 1) * depth] = part[r * depth : (r + 1) * depth]

    attended = tall(attended_ref[...])
    for r in range(2):
        part = dot_tokens(attended, tall(dmid_ref[:, :, r * cols : (r + 1) * cols]).astype(BF16)).astype(BF16)
        for c in range(2):
            dsecond_ref[r, c, depth : 2 * depth] = part[c * depth : (c + 1) * depth]


def whole(shape):
    return pl.BlockSpec(shape, lambda *_: (0,) * len(shape))


def per_image(shape):
    return pl.BlockSpec((1,) + shape, lambda i: (i, 0, 0))


def params():
    return pltpu.CompilerParams(vmem_limit_bytes=VMEM_BYTES)


def cost(flops):
    return pl.CostEstimate(flops=2 * flops, bytes_accessed=20_000_000, transcendentals=2_000_000)


def attend(x, blocks, vec, seq):
    images, rows, width = x.shape
    return pl.pallas_call(
        functools.partial(attend_kernel, seq),
        grid=(images,),
        in_specs=[per_image((rows, width))] + [whole(block.shape) for block in blocks] + [whole(vec.shape)],
        out_specs=[per_image((rows, 3 * width)), per_image((rows, width)), per_image((rows, width))],
        out_shape=[
            jax.ShapeDtypeStruct((images, rows, 3 * width), BF16),
            jax.ShapeDtypeStruct((images, rows, width), BF16),
            jax.ShapeDtypeStruct((images, rows, width), F32),
        ],
        scratch_shapes=[pltpu.VMEM((width, 3 * width), BF16), pltpu.VMEM((width, width), BF16)],
        compiler_params=params(),
        cost_estimate=cost(2 * images * rows * width * (4 * width + 4 * rows)),
        name="attend",
    )(x, *blocks, vec)


def mlp(middle, g, expand, bias, shrink, vec, chunk, carried=None):
    tokens, width = middle.shape
    depth, units = expand[0].shape
    tall = whole(middle.shape)
    expand_specs = [pl.BlockSpec((depth, chunk), lambda j: (0, j))] * 2
    shrink_specs = [pl.BlockSpec((chunk, depth), lambda j: (j, 0))] * 2
    grad_spec = pl.BlockSpec((2, chunk, depth), lambda j: (0, j, 0))
    bias_spec = pl.BlockSpec((1, chunk), lambda j: (0, j))
    grad_shape = jax.ShapeDtypeStruct((2, units, depth), BF16)
    wide = jax.ShapeDtypeStruct((tokens, width), F32)
    grads = [grad_shape, jax.ShapeDtypeStruct(bias.shape, F32), grad_shape]
    grad_specs = [grad_spec, bias_spec, grad_spec]
    scratch = [pltpu.VMEM((tokens, width), BF16)]
    if carried is None:
        carried = ()
        out_specs, out_shape = [tall, tall] + grad_specs, [wide, wide] + grads
    else:
        out_specs = [tall, tall] + grad_specs + [whole((8, width))]
        out_shape = [jax.ShapeDtypeStruct((tokens, width), BF16), wide] + grads + [jax.ShapeDtypeStruct((8, width), F32)]
        scratch = scratch + [pltpu.VMEM((tokens, width), F32)] * 2
    return pl.pallas_call(
        functools.partial(mlp_kernel, len(carried) > 0),
        grid=(units // chunk,),
        in_specs=[tall, tall] + expand_specs + [bias_spec] + shrink_specs + [whole(vec.shape)] + [tall] * len(carried),
        out_specs=out_specs,
        out_shape=out_shape,
        scratch_shapes=scratch,
        compiler_params=params(),
        cost_estimate=cost(12 * tokens * width * units),
        name="mlp",
    )(middle, g, *expand, bias, *shrink, vec, *carried)


def attend_back(x, dmid, qkv, blocks, vec, seq, start, images):
    _, rows, width = x.shape

    def part(last):
        return pl.BlockSpec((images, rows, last), lambda i: (start // images, 0, 0))

    return pl.pallas_call(
        functools.partial(back_kernel, seq),
        grid=(1,),
        in_specs=[part(width), part(width), part(3 * width)] + [whole(block.shape) for block in blocks] + [whole(vec.shape)],
        out_specs=[
            whole((images, rows, width)),
            whole((images, rows, 3 * width)),
            whole((images, rows, width)),
            whole((8, width)),
        ],
        out_shape=[
            jax.ShapeDtypeStruct((images, rows, width), F32),
            jax.ShapeDtypeStruct((images, rows, 3 * width), BF16),
            jax.ShapeDtypeStruct((images, rows, width), BF16),
            jax.ShapeDtypeStruct((8, width), F32),
        ],
        scratch_shapes=[
            pltpu.VMEM((width, 3 * width), BF16),
            pltpu.VMEM((width, width), BF16),
            pltpu.VMEM((rows, width), BF16),
        ],
        compiler_params=params(),
        cost_estimate=cost(2 * images * rows * width * (4 * width + 10 * rows)),
        name="attend_back",
    )(x, dmid, qkv, *blocks, vec)


def attend_weights(normed, dqkv, attended, dmid):
    images, rows, width = attended.shape
    return pl.pallas_call(
        functools.partial(weights_kernel, len(normed)),
        out_shape=[jax.ShapeDtypeStruct((2, 2, width, width // 2), BF16)] * 2,
        compiler_params=params(),
        cost_estimate=cost(2 * images * rows * width * 4 * width),
        name="attend_weights",
    )(*normed, *dqkv, attended, dmid)


def swap(source, axis, bit=0):
    count = lax.axis_size(axis)
    return lax.ppermute(source, axis, [(i, i ^ (1 << bit)) for i in range(count)])


def half_of(source, which, dim=0):
    size = source.shape[dim] // 2
    return lax.dynamic_slice_in_dim(source, which * size, size, dim)


def side(bit):
    return (lax.axis_index("dp") >> bit) & 1


def ordered(mine, other, which, dim=0):
    return jnp.where(
        which == 0, jnp.concatenate([mine, other], dim), jnp.concatenate([other, mine], dim)
    )


def together(chains, outputs=()):
    received, counts = [], []
    for chain in chains:
        sends = chain["sends"]
        counts.append(len(sends))
        received += [swap(*send) for send in sends]
    flat, tree = jax.tree.flatten(outputs)
    held = lax.optimization_barrier(tuple(received) + tuple(flat))
    received, outputs = list(held[: len(received)]), jax.tree.unflatten(tree, held[len(received) :])
    for chain, count in zip(chains, counts):
        mine, received = received[:count], received[count:]
        advance(chain, mine)
    return outputs


def alternate(here, there):
    flying = [[swap(*send) for send in chain["sends"]] for chain in there]
    while any(chain["sends"] for chain in here + there):
        started = [[swap(*send) for send in chain["sends"]] for chain in here]
        ready = [[send[0] for send in chain["sends"]] for chain in here]
        flying, _ = lax.optimization_barrier((flying, ready))
        for chain, received in zip(there, flying):
            if received:
                advance(chain, received)
        here, there, flying = there, here, started


def begin(steps):
    chain = {"steps": steps, "sends": None, "result": None}
    chain["sends"] = next(steps)
    return chain


def advance(chain, received):
    try:
        chain["sends"] = chain["steps"].send(received)
    except StopIteration as stop:
        chain["sends"], chain["result"] = [], stop.value


def bit_count():
    return lax.axis_size("dp").bit_length() - 1


def gather_steps(block):
    if bit_count() > 0:
        at = side(0)
        mine, twin = yield [(half_of(block, at), "col"), (block, "row")]
        (other,) = yield [(mine, "dp")]
        across = ordered(mine, other, at)
    else:
        across, twin = yield [(block, "col"), (block, "row")]
    (twin_across,) = yield [(across, "row")]
    return block, across, twin, twin_across


def sum_steps(parts, col_first):
    total = []
    while len(total) < 2:
        fresh = parts[len(total) :]
        received = yield [(part[1], "row") for part in fresh]
        total += [part[0].astype(F32) + got.astype(F32) for part, got in zip(fresh, received)]
    bits = bit_count()
    order = list(range(bits))
    order.insert(0 if col_first else min(1, bits), "col")
    for bit in order:
        if bit == "col":
            (got,) = yield [(total[1].astype(BF16), "col")]
            total = [total[0] + got.astype(F32)]
        else:
            received = yield [(half_of(one, 1 - side(bit)).astype(BF16), "dp", bit) for one in total]
            total = [half_of(one, side(bit)) + got.astype(F32) for one, got in zip(total, received)]
    total = total[0].astype(BF16)
    for bit in reversed(range(bits)):
        (got,) = yield [(total, "dp", bit)]
        total = ordered(total, got, side(bit))
    return total.astype(F32)


def everywhere_steps(source):
    for axis in ("row", "col"):
        (got,) = yield [(source, axis)]
        source = source + got
    for bit in range(bit_count()):
        (got,) = yield [(source, "dp", bit)]
        source = source + got
    return source


def on_device(
    tokens,
    cotangent,
    triple_weight,
    attend_bias,
    merge_weight,
    expand_weight,
    expand_bias,
    shrink_weight,
    norm_gain,
    norm_shift,
    branch_bias,
):
    images, seq, width = tokens.shape
    rows = -(-seq // 16) * 16
    row_at, col_at = lax.axis_index("row"), lax.axis_index("col")

    def turn(source):
        cut = source.shape[-1] // 2
        return ordered(source[..., :cut], source[..., cut:], row_at, source.ndim - 1)

    pad = ((0, 0), (0, rows - seq), (0, 0))
    x = jnp.pad(turn(tokens), pad)
    g = jnp.pad(turn(cotangent), pad).reshape(images * rows, width)
    biases = jnp.concatenate([attend_bias[0], attend_bias[1], expand_bias]).reshape(1, -1)
    biases = jnp.concatenate([biases, swap(biases, "col")])
    local = attend_bias.shape[1]
    attend_full = [biases[:, t * local : (t + 1) * local].reshape(1, width) for t in range(2)]
    hidden_bias = biases[:, 2 * local :]
    attention = begin(gather_steps(
        jnp.concatenate([triple_weight.transpose(1, 0, 2), merge_weight[None]]).reshape(4 * local, local)
    ))
    x, g, biases = together([attention], (x, g, biases))
    late_expand, late_shrink = lax.optimization_barrier((expand_weight, shrink_weight, attention["sends"][0][0]))[:2]
    late = [begin(gather_steps(late_expand)), begin(gather_steps(late_shrink))]
    pending = [[swap(*send) for send in chain["sends"]] for chain in late]
    while attention["result"] is None:
        together([attention])
    attention = attention["result"]
    filler = jnp.zeros((3, width), F32)
    gain, shift, branch = turn(norm_gain), turn(norm_shift), turn(branch_bias)
    vec_one = jnp.concatenate([gain[0:1], shift[0:1], branch[0:1]] + attend_full + [filler])
    vec_two = jnp.concatenate([gain[1:2], shift[1:2], branch[1:2], filler, filler[:2]])
    pending, (qkv, attended, middle) = lax.optimization_barrier(
        (pending, tuple(attend(x, attention, vec_one, seq)))
    )
    for chain, received in zip(late, pending):
        advance(chain, received)
    middle = middle.reshape(images * rows, width)
    units = expand_bias.shape[0]
    chunk = units // 3
    acc, back, dexpand, dbias, dshrink = together(
        late,
        tuple(mlp(middle, g, (expand_weight, pending[0][1]), hidden_bias[0:1], (shrink_weight, pending[1][1]), vec_two, chunk)),
    )
    while late[0]["result"] is None:
        together(late)
    expand, shrink = late[0]["result"], late[1]["result"]
    sums = [[dshrink], [dexpand]]
    chains = [begin(sum_steps(sums[0], True)), begin(sum_steps(sums[1], False))]
    out, dmid, dexpand, dbias_far, dshrink, sums_two = mlp(
        middle, g, (expand[1], expand[3]), hidden_bias[1:2], (shrink[1], shrink[3]), vec_two, chunk, (acc, back)
    )
    sums[0].append(dshrink)
    sums[1].append(dexpand)
    out, dmid, dbias_far, sums_two = together(chains, (out, dmid, dbias_far, sums_two))
    dmid = dmid.reshape(images, rows, width)
    pieces = 2 if images % 2 == 0 else 1
    count = images // pieces
    done = []
    for piece in range(pieces):
        done.append(together(chains, tuple(attend_back(x, dmid, qkv, attention, vec_one, seq, piece * count, count))))
    dx = jnp.concatenate([held[0] for held in done])
    sums_one = sum(held[3] for held in done)
    dfirst, dsecond = together(
        chains, tuple(attend_weights([held[2] for held in done], [held[1] for held in done], attended, dmid))
    )
    dbias = ordered(dbias, dbias_far, col_at, 1).reshape(-1, width)
    dattend = ordered(sums_one[2:4, :local], sums_one[2:4, local:], col_at, 1)
    shared = jnp.concatenate([turn(sums_one[0:2]), dattend, turn(sums_two[0:4]), dbias])
    chains += [
        begin(sum_steps([dfirst[:, 0], dfirst[:, 1]], True)),
        begin(sum_steps([dsecond[:, 0], dsecond[:, 1]], False)),
        begin(everywhere_steps(shared)),
    ]
    alternate(chains[2:4], chains[0:2] + chains[4:])
    shrink_grad, expand_grad, first, second, shared = [chain["result"] for chain in chains]
    expand_grad = expand_grad.T
    first, second = first.reshape(2, local, local), second.reshape(2, local, local)
    attend_grad = lax.dynamic_slice_in_dim(shared[2:4], col_at * local, local, 1)
    hidden_grad = lax.dynamic_slice_in_dim(shared[8:].reshape(-1), col_at * units, units, 0)
    return (
        turn(out.reshape(images, rows, width)[:, :seq]),
        turn(dx[:, :seq]),
        jnp.stack([first[0], first[1], second[0]], axis=1),
        attend_grad,
        second[1],
        expand_grad,
        hidden_grad,
        shrink_grad,
        jnp.stack([shared[0], shared[4]]),
        jnp.stack([shared[1], shared[5]]),
        shared[6:8],
    )


def solution(mesh):
    placed = (
        P(("dp", "row", "col"), None, None),
        P(("dp", "row", "col"), None, None),
        P("row", None, "col"),
        P(None, "col"),
        P("col", "row"),
        P("row", "col"),
        P("col"),
        P("col", "row"),
        P(),
        P(),
        P(),
    )
    return jax.shard_map(
        on_device,
        mesh=mesh,
        in_specs=placed,
        out_specs=(
            P(("dp", "row", "col"), None, None),
            P(("dp", "row", "col"), None, None),
            P("row", None, "col"),
            P(None, "col"),
            P("col", "row"),
            P("row", "col"),
            P("col"),
            P("col", "row"),
            P(),
            P(),
            P(),
        ),
        check_vma=False,
    )
```

time: 594 us -> 342 us (0.58)
  waiting for transfers between devices: 406 us -> 116 us
  blocking collectives: 58.8 us -> 0 us
  starting transfers between devices: 0.61 us -> 47.4 us
  other arithmetic: 8.7 us -> 31.5 us
  local copies, waits for them, and re-layouts: 11.8 us -> 32.4 us
  Pallas kernels: 93.8 us -> 109 us
  between operations: 14.3 us -> 1.82 us
    reduce_scatter x8 -> x0, waiting for transfers between devices: 178 us -> none  [the longest x4 123 us: owned_total(): mine = lax.psum_scatter(mine, 'col', scatter_dimension=0, tiled=False)]
    all_gather x7 -> x0, waiting for transfers between devices: 131 us -> none  [the longest x3 96.6 us: gather_blocks(): half = lax.all_gather(block, 'col', axis=0, tiled=False)]
    ppermute x0 -> x56, waiting for transfers between devices: none -> 116 us  [swap(): return lax.ppermute(source, axis, [(i, i ^ 1 << bit) for i in range(count)])]
    psum x1 -> x0, waiting for transfers between devices: 92.3 us -> none  [owned_total(): return lax.psum(mine, 'dp').astype(F32)]
    ppermute x0 -> x56, starting transfers between devices: none -> 47.4 us  [swap(): return lax.ppermute(source, axis, [(i, i ^ 1 << bit) for i in range(count)])]
    psum x1 -> x0, blocking collectives: 43.6 us -> none  [on_device(): shared = lax.psum(shared, ('dp', 'row', 'col'))]
    all_gather x2 -> x0, blocking collectives: 15.2 us -> none  [the longest x1 10.7 us: gather_blocks(): half = lax.all_gather(block, 'col', axis=0, tiled=False)]
    pallas_call x2 -> x5, Pallas kernels: 77.8 us -> 92.5 us  [the longest x2 44.4 us: mlp(): pl.pallas_call(functools.partial(mlp_kernel, len(carried) > 0), grid=(uni...]
  transfers between devices with their start and end apart: 16 -> 56, of which waited for: 16 -> 28; matrix products, arithmetic and copies ran while one was open for 2% -> 14% of each run, Pallas kernels for 3% -> 32%
where the time goes in v2:
time: 342 us; the launch traced here: 338 us
  waiting for transfers between devices  116 us (34%)
  Pallas kernels  109 us (32%)
  starting transfers between devices  47.4 us (14%)
  local copies, waits for them, and re-layouts  32.4 us (9%)
  other arithmetic  31.5 us (9%)
    ppermute x56, waiting for transfers between devices, swap(): return lax.ppermute(source, axis, [(i, i ^ 1 << bit) for i in range(count)])  116 us
    ppermute x56, starting transfers between devices, swap(): return lax.ppermute(source, axis, [(i, i ^ 1 << bit) for i in range(count)])  47.4 us
    pallas_call x2, Pallas kernels, mlp(): pl.pallas_call(functools.partial(mlp_kernel, len(carried) > 0), grid=(uni...  44.4 us
    pallas_call x2, Pallas kernels, attend_back(): pl.pallas_call(functools.partial(back_kernel, seq), grid=(1,), in_specs=[...  36.7 us
    pallas_call x1, Pallas kernels, attend(): pl.pallas_call(functools.partial(attend_kernel, seq), grid=(images,), in_...  16.3 us
    pallas_call x1, Pallas kernels, attend_weights(): pl.pallas_call(functools.partial(weights_kernel, len(normed)), out_shape=...  11.4 us
    unnamed x76, local copies, waits for them, and re-layouts  11.2 us
  transfers between devices with their start and end apart: 56, of which 28 were waited for; matrix products, arithmetic and copies ran while one was open for 14% of the time, Pallas kernels for 32%

profile of v2, /device:TPU:0, one launch (start us, length us, event | category | flops | bytes accessed | tf_op | source)
XLA Modules:
  0.0 338.3 jit_solution(8269586073753810383)
XLA Ops:
  0.7 2.4 pad_maximum_fusion.1
  3.5 1.9 constant_dynamic-slice_fusion.3
  5.5 2.6 collective-permute-start
  13.9 8.4 %collective-permute-done = bf16[768,384]{1,0:T(8,128)(2,1)S(1)} collective-permute-done((bf16[768,384]{1,0:T(8,128)(2,1)}, bf16[768,384]{1,0:T(8,128)(2,1)S(1)}, u32[]{:S(2)}, u32[]{:S(2)}) %collective-permute-start) | collective-permute-done | bytes 589856 | tf_op jit(solution)/shard_map/ppermute | solution.py:350
  22.3 1.7 collective-permute-start.7
  24.1 13.2 %collective-permute-done.7 = bf16[768,384]{1,0:T(8,128)(2,1)S(1)} collective-permute-done((bf16[768,384]{1,0:T(8,128)(2,1)S(1)}, bf16[768,384]{1,0:T(8,128)(2,1)S(1)}, u32[]{:S(2)}, u32[]{:S(2)}) %collective-permute-start.7) | collective-permute-done | bytes 589856 | tf_op jit(solution)/shard_map/ppermute | solution.py:350
  42.2 1.6 collective-permute-start.5
  44.4 16.3 %attend.1 = (bf16[4,208,2304]{2,1,0:T(8,128)(2,1)}, bf16[4,208,768]{2,1,0:T(8,128)(2,1)}, f32[4,208,768]{2,1,0:T(8,128)}) custom-call(bf16[4,208,768]{2,1,0:T(8,128)(2,1)} %pad.7.x_ref, bf16[1536,384]{1,0:T(8,128)(2,1)} %bitcast.2.own, bf16[1536,384]{1,0:T(8,128)(2,1)} %copy-done.14, bf16[1536,384]{1,0:T(8,128)(2,1)} %collective-permute-done.1.twin, ...), custom_call_target="tpu_custom_call" | custom-call | flops 9978249216 | bytes 20000000 | tf_op jit(solution)/shard_map/attend/pallas_call | solution.py:254
  60.7 9.8 %collective-permute-done.3 = bf16[192,1536]{1,0:T(8,128)(2,1)S(1)} collective-permute-done((bf16[192,1536]{1,0:T(8,128)(2,1)S(1)}, bf16[192,1536]{1,0:T(8,128)(2,1)S(1)}, u32[]{:S(2)}, u32[]{:S(2)}) %collective-permute-start.3) | collective-permute-done | bytes 589856 | tf_op jit(solution)/shard_map/ppermute | solution.py:350
  70.5 1.6 collective-permute-start.10
  72.6 19.5 %mlp.2 = (f32[832,768]{1,0:T(8,128)}, f32[832,768]{1,0:T(8,128)}, bf16[2,1536,384]{2,1,0:T(8,128)(2,1)}, f32[1,1536]{1,0:T(1,128)}, bf16[2,1536,384]{2,1,0:T(8,128)(2,1)}) custom-call(f32[832,768]{1,0:T(8,128)} %bitcast.71, bf16[832,768]{1,0:T(8,128)(2,1)} %bitcast.65, bf16[384,1536]{1,0:T(8,128)(2,1)} %e0.1, bf16[384,1536]{1,0:T(8,128)(2,1)} %copy-done.31, ...), custom_call_target="tpu_custom_call" | custom-call | flops 23555211264 | bytes 20000000 | tf_op jit(solution)/shard_map/mlp/pallas_call | solution.py:291
  92.1 6.0 %collective-permute-done.9 = bf16[192,1536]{1,0:T(8,128)(2,1)S(1)} collective-permute-done((bf16[192,1536]{1,0:T(8,128)(2,1)S(1)}, bf16[192,1536]{1,0:T(8,128)(2,1)S(1)}, u32[]{:S(2)}, u32[]{:S(2)}) %collective-permute-start.9) | collective-permute-done | bytes 589856 | tf_op jit(solution)/shard_map/ppermute | solution.py:350
  103.5 24.9 %mlp.3 = (bf16[832,768]{1,0:T(8,128)(2,1)}, f32[832,768]{1,0:T(8,128)}, bf16[2,1536,384]{2,1,0:T(8,128)(2,1)}, f32[1,1536]{1,0:T(1,128)}, bf16[2,1536,384]{2,1,0:T(8,128)(2,1)}, /*index=5*/f32[8,768]{1,0:T(8,128)}) custom-call(f32[832,768]{1,0:T(8,128)} %bitcast.72, bf16[832,768]{1,0:T(8,128)(2,1)} %bitcast.66, bf16[384,1536]{1,0:T(8,128)(2,1)} %maximum_select_fusion.3.e0, ...), custom_call_target="tpu_custom_call" | custom-call | flops 23555211264 | bytes 20000000 | tf_op jit(solution)/shard_map/mlp/pallas_call | solution.py:291
  128.5 3.3 slice_bitcast_fusion.1
  133.5 1.6 convert_add_fusion.2
  140.5 2.8 copy.28
  143.3 18.4 %attend_back.2 = (f32[2,208,768]{2,1,0:T(8,128)}, bf16[2,208,2304]{2,1,0:T(8,128)(2,1)}, bf16[2,208,768]{2,1,0:T(8,128)(2,1)}, f32[8,768]{1,0:T(8,128)}) custom-call(bf16[4,208,768]{2,1,0:T(8,128)(2,1)} %pad.7.x_ref, f32[4,208,768]{2,1,0:T(8,128)} %bitcast.73, bf16[4,208,2304]{2,1,0:T(8,128)(2,1)} %get-tuple-element.149.qkv_ref, ...), custom_call_target="tpu_custom_call" | custom-call | flops 6584008704 | bytes 20000000 | tf_op jit(solution)/shard_map/attend_back/pallas_call | solution.py:310
  166.9 18.4 %attend_back.3 = (f32[2,208,768]{2,1,0:T(8,128)}, bf16[2,208,2304]{2,1,0:T(8,128)(2,1)}, bf16[2,208,768]{2,1,0:T(8,128)(2,1)}, f32[8,768]{1,0:T(8,128)}) custom-call(bf16[4,208,768]{2,1,0:T(8,128)(2,1)} %pad.7.x_ref, f32[4,208,768]{2,1,0:T(8,128)} %bitcast.74, bf16[4,208,2304]{2,1,0:T(8,128)(2,1)} %get-tuple-element.149.qkv_ref, ...), custom_call_target="tpu_custom_call" | custom-call | flops 6584008704 | bytes 20000000 | tf_op jit(solution)/shard_map/attend_back/pallas_call | solution.py:310
  185.2 6.0 %collective-permute-done.17 = bf16[1536,384]{1,0:T(8,128)(2,1)} collective-permute-done((bf16[1536,384]{1,0:T(8,128)(2,1)}, bf16[1536,384]{1,0:T(8,128)(2,1)}, u32[]{:S(2)}, u32[]{:S(2)}) %collective-permute-start.17) | collective-permute-done | bytes 1179680 | tf_op jit(solution)/shard_map/ppermute | solution.py:350
  193.3 2.1 add_convert_fusion
  196.9 1.7 fusion
  199.2 11.4 %attend_weights.1 = (bf16[2,2,768,384]{3,2,1,0:T(8,128)(2,1)}, bf16[2,2,768,384]{3,2,1,0:T(8,128)(2,1)}) custom-call(bf16[2,208,768]{2,1,0:T(8,128)(2,1)} %get-tuple-element.166.refs_0_, bf16[2,208,768]{2,1,0:T(8,128)(2,1)} %get-tuple-element.167.refs_1_, bf16[2,208,2304]{2,1,0:T(8,128)(2,1)} %get-tuple-element.168.refs_2_, ...), custom_call_target="tpu_custom_call" | custom-call | flops 7851737088 | bytes 20000000 | tf_op jit(solution)/shard_map/attend_weights/pallas_call | solution.py:339
  211.3 2.7 collective-permute-done.20
  215.5 1.6 collective-permute-start.27
  219.8 5.8 %collective-permute-done.27 = bf16[384,384]{1,0:T(8,128)(2,1)S(1)} collective-permute-done((bf16[384,384]{1,0:T(8,128)(2,1)S(1)}, bf16[384,384]{1,0:T(8,128)(2,1)S(1)}, u32[]{:S(2)}, u32[]{:S(2)}) %collective-permute-start.27) | collective-permute-done | bytes 294944 | tf_op jit(solution)/shard_map/ppermute | solution.py:350
  225.5 4.6 %collective-permute-done.26 = bf16[384,384]{1,0:T(8,128)(2,1)S(1)} collective-permute-done((bf16[384,384]{1,0:T(8,128)(2,1)S(1)}, bf16[384,384]{1,0:T(8,128)(2,1)S(1)}, u32[]{:S(2)}, u32[]{:S(2)}) %collective-permute-start.26) | collective-permute-done | bytes 294944 | tf_op jit(solution)/shard_map/ppermute | solution.py:350
  230.3 2.7 collective-permute-start.33
  239.1 3.7 %collective-permute-done.33 = bf16[192,384]{1,0:T(8,128)(2,1)S(1)} collective-permute-done((bf16[192,384]{1,0:T(8,128)(2,1)S(1)}, bf16[192,384]{1,0:T(8,128)(2,1)S(1)}, u32[]{:S(2)}, u32[]{:S(2)}) %collective-permute-start.33) | collective-permute-done | bytes 147488 | tf_op jit(solution)/shard_map/ppermute | solution.py:350
  242.9 2.0 collective-permute-done.32
  246.8 2.1 collective-permute-start.37
  251.9 6.5 %collective-permute-done.38 = bf16[192,384]{1,0:T(8,128)(2,1)S(1)} collective-permute-done((bf16[192,384]{1,0:T(8,128)(2,1)S(1)}, bf16[192,384]{1,0:T(8,128)(2,1)S(1)}, u32[]{:S(2)}, u32[]{:S(2)}) %collective-permute-start.38) | collective-permute-done | bytes 147488 | tf_op jit(solution)/shard_map/ppermute | solution.py:350
  260.2 2.0 collective-permute-start.44
  262.7 2.0 collective-permute-start.41
  264.8 6.4 %collective-permute-done.44 = f32[12,768]{1,0:T(8,128)S(1)} collective-permute-done((f32[12,768]{1,0:T(8,128)S(1)}, f32[12,768]{1,0:T(8,128)S(1)}, u32[]{:S(2)}, u32[]{:S(2)}) %collective-permute-start.44) | collective-permute-done | bytes 36896 | tf_op jit(solution)/shard_map/ppermute | solution.py:350
  271.2 6.3 %collective-permute-done.42 = bf16[384,384]{1,0:T(8,128)(2,1)S(1)} collective-permute-done((bf16[384,384]{1,0:T(8,128)(2,1)S(1)}, bf16[384,384]{1,0:T(8,128)(2,1)S(1)}, u32[]{:S(2)}, u32[]{:S(2)}) %collective-permute-start.42) | collective-permute-done | bytes 294944 | tf_op jit(solution)/shard_map/ppermute | solution.py:350
  281.0 2.2 collective-permute-start.46
  284.1 4.3 %collective-permute-done.46 = bf16[96,384]{1,0:T(8,128)(2,1)S(1)} collective-permute-done((bf16[96,384]{1,0:T(8,128)(2,1)S(1)}, bf16[96,384]{1,0:T(8,128)(2,1)S(1)}, u32[]{:S(2)}, u32[]{:S(2)}) %collective-permute-start.46) | collective-permute-done | bytes 73760 | tf_op jit(solution)/shard_map/ppermute | solution.py:350
  288.4 1.9 collective-permute-done.45
  290.4 3.0 collective-permute-start.47
  293.9 1.8 collective-permute-start.53
  295.6 3.4 %collective-permute-done.48 = bf16[96,384]{1,0:T(8,128)(2,1)S(1)} collective-permute-done((bf16[96,384]{1,0:T(8,128)(2,1)S(1)}, bf16[96,384]{1,0:T(8,128)(2,1)S(1)}, u32[]{:S(2)}, u32[]{:S(2)}) %collective-permute-start.48) | collective-permute-done | bytes 73760 | tf_op jit(solution)/shard_map/ppermute | solution.py:350
  299.9 2.1 collective-permute-start.49
  302.3 2.6 copy.29
  306.4 2.1 collective-permute-done.49
  308.8 2.1 collective-permute-start.51
  310.8 11.8 %collective-permute-done.53 = bf16[768,384]{1,0:T(8,128)(2,1)} collective-permute-done((bf16[768,384]{1,0:T(8,128)(2,1)S(1)}, bf16[768,384]{1,0:T(8,128)(2,1)}, u32[]{:S(2)}, u32[]{:S(2)}) %collective-permute-start.53) | collective-permute-done | bytes 589856 | tf_op jit(solution)/shard_map/ppermute | solution.py:350
  324.0 2.0 copy.30
  330.5 2.9 fusion.2
  (259 shorter events, 70.4 us)
Async XLA Ops:
  3.1 19.2 %collective-permute-start.1 = (bf16[1536,384]{1,0:T(8,128)(2,1)}, bf16[1536,384]{1,0:T(8,128)(2,1)}, u32[]{:S(2)}, u32[]{:S(2)}) collective-permute-start(bf16[1536,384]{1,0:T(8,128)(2,1)} %bitcast.2.own), channel_id=1, source_target_pairs={{0,2},{2,0},{1,3},{3,1},{4,6},{6,4},{5,7},{7,5},{8,10},{10,8},{9,1... | collective-permute-start | bytes 3538952 | tf_op jit(solution)/shard_map/ppermute | solution.py:350
  5.5 16.8 %collective-permute-start = (bf16[768,384]{1,0:T(8,128)(2,1)}, bf16[768,384]{1,0:T(8,128)(2,1)S(1)}, u32[]{:S(2)}, u32[]{:S(2)}) collective-permute-start(bf16[768,384]{1,0:T(8,128)(2,1)} %constant_dynamic-slice_fusion.3), channel_id=1, source_target_pairs={{0,1},{1,0},{2,3},{3,2},{4,5},{5,4},{6,7},{7,6},{8,9},{9,8},{10,11... | collective-permute-start | bytes 1769480 | tf_op jit(solution)/shard_map/ppermute | solution.py:350
  8.2 30.9 %collective-permute-start.2 = (f32[1,2304]{1,0:T(1,128)S(1)}, f32[1,2304]{1,0:T(1,128)}, u32[]{:S(2)}, u32[]{:S(2)}) collective-permute-start(f32[1,2304]{1,0:T(1,128)S(1)} %reshape.111), channel_id=1, source_target_pairs={{0,1},{1,0},{2,3},{3,2},{4,5},{5,4},{6,7},{7,6},{8,9},{9,8},{10,11... | collective-permute-start | bytes 27656 | tf_op jit(solution)/shard_map/ppermute | solution.py:350
  22.3 15.0 %collective-permute-start.7 = (bf16[768,384]{1,0:T(8,128)(2,1)S(1)}, bf16[768,384]{1,0:T(8,128)(2,1)S(1)}, u32[]{:S(2)}, u32[]{:S(2)}) collective-permute-start(bf16[768,384]{1,0:T(8,128)(2,1)S(1)} %collective-permute-done), channel_id=1, source_target_pairs={{0,4},{4,0},{8,12},{12,8},{16,20},{20,16},{24,28},{28,24},{1,5},{5... | collective-permute-start | bytes 1769480 | tf_op jit(solution)/shard_map/ppermute | solution.py:350
  40.5 30.1 %collective-permute-start.4 = (bf16[384,1536]{1,0:T(8,128)(2,1)}, bf16[384,1536]{1,0:T(8,128)(2,1)S(1)}, u32[]{:S(2)}, u32[]{:S(2)}) collective-permute-start(bf16[384,1536]{1,0:T(8,128)(2,1)} %e0.1), channel_id=1, source_target_pairs={{0,2},{2,0},{1,3},{3,1},{4,6},{6,4},{5,7},{7,5},{8,10},{10,8},{9,1... | collective-permute-start | bytes 3538952 | tf_op jit(solution)/shard_map/ppermute | solution.py:350
  42.1 28.5 %collective-permute-start.6 = (bf16[1536,384]{1,0:T(8,128)(2,1)}, bf16[1536,384]{1,0:T(8,128)(2,1)S(1)}, u32[]{:S(2)}, u32[]{:S(2)}) collective-permute-start(bf16[1536,384]{1,0:T(8,128)(2,1)} %s0.1), channel_id=1, source_target_pairs={{0,2},{2,0},{1,3},{3,1},{4,6},{6,4},{5,7},{7,5},{8,10},{10,8},{9,1... | collective-permute-start | bytes 3538952 | tf_op jit(solution)/shard_map/ppermute | solution.py:350
  42.2 18.5 %collective-permute-start.5 = (bf16[768,384]{1,0:T(8,128)(2,1)S(1)}, bf16[768,384]{1,0:T(8,128)(2,1)S(1)}, u32[]{:S(2)}, u32[]{:S(2)}) collective-permute-start(bf16[768,384]{1,0:T(8,128)(2,1)S(1)} %constant_dynamic-slice_fusion.1), channel_id=1, source_target_pairs={{0,1},{1,0},{2,3},{3,2},{4,5},{5,4},{6,7},{7,6},{8,9},{9,8},{10,11... | collective-permute-start | bytes 1769480 | tf_op jit(solution)/shard_map/ppermute | solution.py:350
  43.8 26.7 %collective-permute-start.3 = (bf16[192,1536]{1,0:T(8,128)(2,1)S(1)}, bf16[192,1536]{1,0:T(8,128)(2,1)S(1)}, u32[]{:S(2)}, u32[]{:S(2)}) collective-permute-start(bf16[192,1536]{1,0:T(8,128)(2,1)S(1)} %constant_dynamic-slice_fusion.2), channel_id=1, source_target_pairs={{0,1},{1,0},{2,3},{3,2},{4,5},{5,4},{6,7},{7,6},{8,9},{9,8},{10,11... | collective-permute-start | bytes 1769480 | tf_op jit(solution)/shard_map/ppermute | solution.py:350
  70.5 21.6 %collective-permute-start.10 = (bf16[768,384]{1,0:T(8,128)(2,1)S(1)}, bf16[768,384]{1,0:T(8,128)(2,1)S(1)}, u32[]{:S(2)}, u32[]{:S(2)}) collective-permute-start(bf16[768,384]{1,0:T(8,128)(2,1)S(1)} %collective-permute-done.5), channel_id=1, source_target_pairs={{0,4},{4,0},{8,12},{12,8},{16,20},{20,16},{24,28},{28,24},{1,5},{5... | collective-permute-start | bytes 1769480 | tf_op jit(solution)/shard_map/ppermute | solution.py:350
  72.2 26.0 %collective-permute-start.9 = (bf16[192,1536]{1,0:T(8,128)(2,1)S(1)}, bf16[192,1536]{1,0:T(8,128)(2,1)S(1)}, u32[]{:S(2)}, u32[]{:S(2)}) collective-permute-start(bf16[192,1536]{1,0:T(8,128)(2,1)S(1)} %collective-permute-done.3), channel_id=1, source_target_pairs={{0,4},{4,0},{8,12},{12,8},{16,20},{20,16},{24,28},{28,24},{1,5},{5... | collective-permute-start | bytes 1769480 | tf_op jit(solution)/shard_map/ppermute | solution.py:350
  102.1 26.4 %collective-permute-start.11 = (bf16[1536,384]{1,0:T(8,128)(2,1)S(1)}, bf16[1536,384]{1,0:T(8,128)(2,1)S(1)}, u32[]{:S(2)}, u32[]{:S(2)}) collective-permute-start(bf16[1536,384]{1,0:T(8,128)(2,1)S(1)} %slice_bitcast_fusion.3), channel_id=1, source_target_pairs={{0,2},{2,0},{1,3},{3,1},{4,6},{6,4},{5,7},{7,5},{8,10},{10,8},{9,1... | collective-permute-start | bytes 3538952 | tf_op jit(solution)/shard_map/ppermute | solution.py:350
  102.5 26.0 %collective-permute-start.12 = (bf16[1536,384]{1,0:T(8,128)(2,1)S(1)}, bf16[1536,384]{1,0:T(8,128)(2,1)S(1)}, u32[]{:S(2)}, u32[]{:S(2)}) collective-permute-start(bf16[1536,384]{1,0:T(8,128)(2,1)S(1)} %slice_bitcast_fusion.2), channel_id=1, source_target_pairs={{0,2},{2,0},{1,3},{3,1},{4,6},{6,4},{5,7},{7,5},{8,10},{10,8},{9,1... | collective-permute-start | bytes 3538952 | tf_op jit(solution)/shard_map/ppermute | solution.py:350
  131.8 29.9 %collective-permute-start.15 = (bf16[1536,384]{1,0:T(8,128)(2,1)}, bf16[1536,384]{1,0:T(8,128)(2,1)S(1)}, u32[]{:S(2)}, u32[]{:S(2)}) collective-permute-start(bf16[1536,384]{1,0:T(8,128)(2,1)} %slice_bitcast_fusion.1), channel_id=1, source_target_pairs={{0,2},{2,0},{1,3},{3,1},{4,6},{6,4},{5,7},{7,5},{8,10},{10,8},{9,1... | collective-permute-start | bytes 3538952 | tf_op jit(solution)/shard_map/ppermute | solution.py:350
  133.2 28.5 %collective-permute-start.16 = (bf16[1536,384]{1,0:T(8,128)(2,1)}, bf16[1536,384]{1,0:T(8,128)(2,1)}, u32[]{:S(2)}, u32[]{:S(2)}) collective-permute-start(bf16[1536,384]{1,0:T(8,128)(2,1)} %slice_bitcast_fusion), channel_id=1, source_target_pairs={{0,2},{2,0},{1,3},{3,1},{4,6},{6,4},{5,7},{7,5},{8,10},{10,8},{9,1... | collective-permute-start | bytes 3538952 | tf_op jit(solution)/shard_map/ppermute | solution.py:350
  136.0 49.2 %collective-permute-start.18 = (bf16[768,384]{1,0:T(8,128)(2,1)}, bf16[768,384]{1,0:T(8,128)(2,1)}, u32[]{:S(2)}, u32[]{:S(2)}) collective-permute-start(bf16[768,384]{1,0:T(8,128)(2,1)} %dynamic-slice_convert_fusion.2), channel_id=1, source_target_pairs={{0,4},{4,0},{8,12},{12,8},{16,20},{20,16},{24,28},{28,24},{1,5},{5... | collective-permute-start | bytes 1769480 | tf_op jit(solution)/shard_map/ppermute | solution.py:350
  163.1 28.1 %collective-permute-start.17 = (bf16[1536,384]{1,0:T(8,128)(2,1)}, bf16[1536,384]{1,0:T(8,128)(2,1)}, u32[]{:S(2)}, u32[]{:S(2)}) collective-permute-start(bf16[1536,384]{1,0:T(8,128)(2,1)} %fusion.1), channel_id=1, source_target_pairs={{0,1},{1,0},{2,3},{3,2},{4,5},{5,4},{6,7},{7,6},{8,9},{9,8},{10,11... | collective-permute-start | bytes 3538952 | tf_op jit(solution)/shard_map/ppermute | solution.py:350
  166.3 19.0 %collective-permute-start.19 = (bf16[768,384]{1,0:T(8,128)(2,1)S(1)}, bf16[768,384]{1,0:T(8,128)(2,1)}, u32[]{:S(2)}, u32[]{:S(2)}) collective-permute-start(bf16[768,384]{1,0:T(8,128)(2,1)S(1)} %dynamic-slice_convert_fusion.1), channel_id=1, source_target_pairs={{0,4},{4,0},{8,12},{12,8},{16,20},{20,16},{24,28},{28,24},{1,5},{5... | collective-permute-start | bytes 1769480 | tf_op jit(solution)/shard_map/ppermute | solution.py:350
  193.3 26.4 %collective-permute-start.28 = (f32[12,768]{1,0:T(8,128)}, f32[12,768]{1,0:T(8,128)}, u32[]{:S(2)}, u32[]{:S(2)}) collective-permute-start(f32[12,768]{1,0:T(8,128)} %pad_maximum_fusion.2), channel_id=1, source_target_pairs={{0,2},{2,0},{1,3},{3,1},{4,6},{6,4},{5,7},{7,5},{8,10},{10,8},{9,1... | collective-permute-start | bytes 110600 | tf_op jit(solution)/shard_map/ppermute | solution.py:350
  195.3 16.0 %collective-permute-start.21 = (bf16[768,384]{1,0:T(8,128)(2,1)}, bf16[768,384]{1,0:T(8,128)(2,1)}, u32[]{:S(2)}, u32[]{:S(2)}) collective-permute-start(bf16[768,384]{1,0:T(8,128)(2,1)} %add_convert_fusion), channel_id=1, source_target_pairs={{0,1},{1,0},{2,3},{3,2},{4,5},{5,4},{6,7},{7,6},{8,9},{9,8},{10,11... | collective-permute-start | bytes 1769480 | tf_op jit(solution)/shard_map/ppermute | solution.py:350
  198.6 15.5 %collective-permute-start.20 = (bf16[768,384]{1,0:T(8,128)(2,1)S(1)}, bf16[768,384]{1,0:T(8,128)(2,1)S(1)}, u32[]{:S(2)}, u32[]{:S(2)}) collective-permute-start(bf16[768,384]{1,0:T(8,128)(2,1)S(1)} %dynamic-slice_convert_fusion), channel_id=1, source_target_pairs={{0,4},{4,0},{8,12},{12,8},{16,20},{20,16},{24,28},{28,24},{1,5},{5... | collective-permute-start | bytes 1769480 | tf_op jit(solution)/shard_map/ppermute | solution.py:350
  215.5 10.0 %collective-permute-start.27 = (bf16[384,384]{1,0:T(8,128)(2,1)S(1)}, bf16[384,384]{1,0:T(8,128)(2,1)S(1)}, u32[]{:S(2)}, u32[]{:S(2)}) collective-permute-start(bf16[384,384]{1,0:T(8,128)(2,1)S(1)} %dynamic-slice_convert_fusion.6), channel_id=1, source_target_pairs={{0,8},{4,12},{8,0},{12,4},{16,24},{20,28},{24,16},{28,20},{1,9},{5... | collective-permute-start | bytes 884744 | tf_op jit(solution)/shard_map/ppermute | solution.py:350
  217.3 12.8 %collective-permute-start.26 = (bf16[384,384]{1,0:T(8,128)(2,1)S(1)}, bf16[384,384]{1,0:T(8,128)(2,1)S(1)}, u32[]{:S(2)}, u32[]{:S(2)}) collective-permute-start(bf16[384,384]{1,0:T(8,128)(2,1)S(1)} %dynamic-slice_convert_fusion.7), channel_id=1, source_target_pairs={{0,8},{4,12},{8,0},{12,4},{16,24},{20,28},{24,16},{28,20},{1,9},{5... | collective-permute-start | bytes 884744 | tf_op jit(solution)/shard_map/ppermute | solution.py:350
  219.1 14.7 %collective-permute-start.22 = (bf16[768,384]{1,0:T(8,128)(2,1)S(1)}, bf16[768,384]{1,0:T(8,128)(2,1)S(1)}, u32[]{:S(2)}, u32[]{:S(2)}) collective-permute-start(bf16[768,384]{1,0:T(8,128)(2,1)S(1)} %get-tuple-element.237), channel_id=1, source_target_pairs={{0,2},{2,0},{1,3},{3,1},{4,6},{6,4},{5,7},{7,5},{8,10},{10,8},{9,1... | collective-permute-start | bytes 1769480 | tf_op jit(solution)/shard_map/ppermute | solution.py:350
  219.2 15.2 %collective-permute-start.23 = (bf16[768,384]{1,0:T(8,128)(2,1)S(1)}, bf16[768,384]{1,0:T(8,128)(2,1)S(1)}, u32[]{:S(2)}, u32[]{:S(2)}) collective-permute-start(bf16[768,384]{1,0:T(8,128)(2,1)S(1)} %get-tuple-element.236), channel_id=1, source_target_pairs={{0,2},{2,0},{1,3},{3,1},{4,6},{6,4},{5,7},{7,5},{8,10},{10,8},{9,1... | collective-permute-start | bytes 1769480 | tf_op jit(solution)/shard_map/ppermute | solution.py:350
  219.7 15.2 %collective-permute-start.24 = (bf16[768,384]{1,0:T(8,128)(2,1)S(1)}, bf16[768,384]{1,0:T(8,128)(2,1)S(1)}, u32[]{:S(2)}, u32[]{:S(2)}) collective-permute-start(bf16[768,384]{1,0:T(8,128)(2,1)S(1)} %get-tuple-element.235), channel_id=1, source_target_pairs={{0,2},{2,0},{1,3},{3,1},{4,6},{6,4},{5,7},{7,5},{8,10},{10,8},{9,1... | collective-permute-start | bytes 1769480 | tf_op jit(solution)/shard_map/ppermute | solution.py:350
  225.5 9.4 %collective-permute-start.25 = (bf16[768,384]{1,0:T(8,128)(2,1)S(1)}, bf16[768,384]{1,0:T(8,128)(2,1)S(1)}, u32[]{:S(2)}, u32[]{:S(2)}) collective-permute-start(bf16[768,384]{1,0:T(8,128)(2,1)S(1)} %get-tuple-element.234), channel_id=1, source_target_pairs={{0,2},{2,0},{1,3},{3,1},{4,6},{6,4},{5,7},{7,5},{8,10},{10,8},{9,1... | collective-permute-start | bytes 1769480 | tf_op jit(solution)/shard_map/ppermute | solution.py:350
  230.3 12.6 %collective-permute-start.33 = (bf16[192,384]{1,0:T(8,128)(2,1)S(1)}, bf16[192,384]{1,0:T(8,128)(2,1)S(1)}, u32[]{:S(2)}, u32[]{:S(2)}) collective-permute-start(bf16[192,384]{1,0:T(8,128)(2,1)S(1)} %dynamic-slice_convert_fusion.10), channel_id=1, source_target_pairs={{0,16},{4,20},{8,24},{12,28},{16,0},{20,4},{24,8},{28,12},{1,17},{... | collective-permute-start | bytes 442376 | tf_op jit(solution)/shard_map/ppermute | solution.py:350
  234.4 10.4 %collective-permute-start.32 = (bf16[192,384]{1,0:T(8,128)(2,1)S(1)}, bf16[192,384]{1,0:T(8,128)(2,1)S(1)}, u32[]{:S(2)}, u32[]{:S(2)}) collective-permute-start(bf16[192,384]{1,0:T(8,128)(2,1)S(1)} %dynamic-slice_convert_fusion.11), channel_id=1, source_target_pairs={{0,16},{4,20},{8,24},{12,28},{16,0},{20,4},{24,8},{28,12},{1,17},{... | collective-permute-start | bytes 442376 | tf_op jit(solution)/shard_map/ppermute | solution.py:350
  235.1 15.3 %collective-permute-start.29 = (bf16[768,384]{1,0:T(8,128)(2,1)S(1)}, bf16[768,384]{1,0:T(8,128)(2,1)S(1)}, u32[]{:S(2)}, u32[]{:S(2)}) collective-permute-start(bf16[768,384]{1,0:T(8,128)(2,1)S(1)} %fusion.3), channel_id=1, source_target_pairs={{0,1},{1,0},{2,3},{3,2},{4,5},{5,4},{6,7},{7,6},{8,9},{9,8},{10,11... | collective-permute-start | bytes 1769480 | tf_op jit(solution)/shard_map/ppermute | solution.py:350
  237.0 9.8 %collective-permute-start.31 = (bf16[384,384]{1,0:T(8,128)(2,1)S(1)}, bf16[384,384]{1,0:T(8,128)(2,1)S(1)}, u32[]{:S(2)}, u32[]{:S(2)}) collective-permute-start(bf16[384,384]{1,0:T(8,128)(2,1)S(1)} %dynamic-slice_convert_fusion.4), channel_id=1, source_target_pairs={{0,4},{4,0},{8,12},{12,8},{16,20},{20,16},{24,28},{28,24},{1,5},{5... | collective-permute-start | bytes 884744 | tf_op jit(solution)/shard_map/ppermute | solution.py:350
  238.6 11.8 %collective-permute-start.30 = (bf16[384,384]{1,0:T(8,128)(2,1)S(1)}, bf16[384,384]{1,0:T(8,128)(2,1)S(1)}, u32[]{:S(2)}, u32[]{:S(2)}) collective-permute-start(bf16[384,384]{1,0:T(8,128)(2,1)S(1)} %dynamic-slice_convert_fusion.5), channel_id=1, source_target_pairs={{0,4},{4,0},{8,12},{12,8},{16,20},{20,16},{24,28},{28,24},{1,5},{5... | collective-permute-start | bytes 884744 | tf_op jit(solution)/shard_map/ppermute | solution.py:350
  244.9 13.6 %collective-permute-start.38 = (bf16[192,384]{1,0:T(8,128)(2,1)S(1)}, bf16[192,384]{1,0:T(8,128)(2,1)S(1)}, u32[]{:S(2)}, u32[]{:S(2)}) collective-permute-start(bf16[192,384]{1,0:T(8,128)(2,1)S(1)} %add_convert_fusion.2), channel_id=1, source_target_pairs={{0,16},{4,20},{8,24},{12,28},{16,0},{20,4},{24,8},{28,12},{1,17},{... | collective-permute-start | bytes 442376 | tf_op jit(solution)/shard_map/ppermute | solution.py:350
  246.8 13.3 %collective-permute-start.37 = (bf16[192,384]{1,0:T(8,128)(2,1)S(1)}, bf16[192,384]{1,0:T(8,128)(2,1)S(1)}, u32[]{:S(2)}, u32[]{:S(2)}) collective-permute-start(bf16[192,384]{1,0:T(8,128)(2,1)S(1)} %add_convert_fusion.3), channel_id=1, source_target_pairs={{0,16},{4,20},{8,24},{12,28},{16,0},{20,4},{24,8},{28,12},{1,17},{... | collective-permute-start | bytes 442376 | tf_op jit(solution)/shard_map/ppermute | solution.py:350
  250.7 11.7 %collective-permute-start.36 = (bf16[384,384]{1,0:T(8,128)(2,1)S(1)}, bf16[384,384]{1,0:T(8,128)(2,1)S(1)}, u32[]{:S(2)}, u32[]{:S(2)}) collective-permute-start(bf16[384,384]{1,0:T(8,128)(2,1)S(1)} %add_convert_fusion.1), channel_id=1, source_target_pairs={{0,1},{1,0},{2,3},{3,2},{4,5},{5,4},{6,7},{7,6},{8,9},{9,8},{10,11... | collective-permute-start | bytes 884744 | tf_op jit(solution)/shard_map/ppermute | solution.py:350
  251.3 11.2 %collective-permute-start.35 = (bf16[384,384]{1,0:T(8,128)(2,1)S(1)}, bf16[384,384]{1,0:T(8,128)(2,1)S(1)}, u32[]{:S(2)}, u32[]{:S(2)}) collective-permute-start(bf16[384,384]{1,0:T(8,128)(2,1)S(1)} %dynamic-slice_convert_fusion.3), channel_id=1, source_target_pairs={{0,4},{4,0},{8,12},{12,8},{16,20},{20,16},{24,28},{28,24},{1,5},{5... | collective-permute-start | bytes 884744 | tf_op jit(solution)/shard_map/ppermute | solution.py:350
  260.1 11.1 %collective-permute-start.43 = (bf16[384,384]{1,0:T(8,128)(2,1)S(1)}, bf16[384,384]{1,0:T(8,128)(2,1)S(1)}, u32[]{:S(2)}, u32[]{:S(2)}) collective-permute-start(bf16[384,384]{1,0:T(8,128)(2,1)S(1)} %maximum_select_fusion.12), channel_id=1, source_target_pairs={{0,8},{4,12},{8,0},{12,4},{16,24},{20,28},{24,16},{28,20},{1,9},{5... | collective-permute-start | bytes 884744 | tf_op jit(solution)/shard_map/ppermute | solution.py:350
  260.2 11.0 %collective-permute-start.44 = (f32[12,768]{1,0:T(8,128)S(1)}, f32[12,768]{1,0:T(8,128)S(1)}, u32[]{:S(2)}, u32[]{:S(2)}) collective-permute-start(f32[12,768]{1,0:T(8,128)S(1)} %add.194), channel_id=1, source_target_pairs={{0,8},{4,12},{8,0},{12,4},{16,24},{20,28},{24,16},{28,20},{1,9},{5... | collective-permute-start | bytes 110600 | tf_op jit(solution)/shard_map/ppermute | solution.py:350
  262.3 15.2 %collective-permute-start.42 = (bf16[384,384]{1,0:T(8,128)(2,1)S(1)}, bf16[384,384]{1,0:T(8,128)(2,1)S(1)}, u32[]{:S(2)}, u32[]{:S(2)}) collective-permute-start(bf16[384,384]{1,0:T(8,128)(2,1)S(1)} %maximum_select_fusion.11), channel_id=1, source_target_pairs={{0,8},{4,12},{8,0},{12,4},{16,24},{20,28},{24,16},{28,20},{1,9},{5... | collective-permute-start | bytes 884744 | tf_op jit(solution)/shard_map/ppermute | solution.py:350
  262.7 16.6 %collective-permute-start.41 = (bf16[192,384]{1,0:T(8,128)(2,1)S(1)}, bf16[192,384]{1,0:T(8,128)(2,1)S(1)}, u32[]{:S(2)}, u32[]{:S(2)}) collective-permute-start(bf16[192,384]{1,0:T(8,128)(2,1)S(1)} %dynamic-slice_convert_fusion.8), channel_id=1, source_target_pairs={{0,8},{4,12},{8,0},{12,4},{16,24},{20,28},{24,16},{28,20},{1,9},{5... | collective-permute-start | bytes 442376 | tf_op jit(solution)/shard_map/ppermute | solution.py:350
  264.7 16.1 %collective-permute-start.40 = (bf16[192,384]{1,0:T(8,128)(2,1)S(1)}, bf16[192,384]{1,0:T(8,128)(2,1)S(1)}, u32[]{:S(2)}, u32[]{:S(2)}) collective-permute-start(bf16[192,384]{1,0:T(8,128)(2,1)S(1)} %dynamic-slice_convert_fusion.9), channel_id=1, source_target_pairs={{0,8},{4,12},{8,0},{12,4},{16,24},{20,28},{24,16},{28,20},{1,9},{5... | collective-permute-start | bytes 442376 | tf_op jit(solution)/shard_map/ppermute | solution.py:350
  281.0 7.4 %collective-permute-start.46 = (bf16[96,384]{1,0:T(8,128)(2,1)S(1)}, bf16[96,384]{1,0:T(8,128)(2,1)S(1)}, u32[]{:S(2)}, u32[]{:S(2)}) collective-permute-start(bf16[96,384]{1,0:T(8,128)(2,1)S(1)} %dynamic-slice_convert_fusion.12), channel_id=1, source_target_pairs={{0,16},{4,20},{8,24},{12,28},{16,0},{20,4},{24,8},{28,12},{1,17},{... | collective-permute-start | bytes 221192 | tf_op jit(solution)/shard_map/ppermute | solution.py:350
  290.3 8.7 %collective-permute-start.48 = (bf16[96,384]{1,0:T(8,128)(2,1)S(1)}, bf16[96,384]{1,0:T(8,128)(2,1)S(1)}, u32[]{:S(2)}, u32[]{:S(2)}) collective-permute-start(bf16[96,384]{1,0:T(8,128)(2,1)S(1)} %add_convert_fusion.4), channel_id=1, source_target_pairs={{0,16},{4,20},{8,24},{12,28},{16,0},{20,4},{24,8},{28,12},{1,17},{... | collective-permute-start | bytes 221192 | tf_op jit(solution)/shard_map/ppermute | solution.py:350
  290.4 9.4 %collective-permute-start.47 = (bf16[96,384]{1,0:T(8,128)(2,1)S(1)}, bf16[96,384]{1,0:T(8,128)(2,1)S(1)}, u32[]{:S(2)}, u32[]{:S(2)}) collective-permute-start(bf16[96,384]{1,0:T(8,128)(2,1)S(1)} %add_convert_fusion.5), channel_id=1, source_target_pairs={{0,16},{4,20},{8,24},{12,28},{16,0},{20,4},{24,8},{28,12},{1,17},{... | collective-permute-start | bytes 221192 | tf_op jit(solution)/shard_map/ppermute | solution.py:350
  293.5 17.3 %collective-permute-start.54 = (bf16[768,384]{1,0:T(8,128)(2,1)S(1)}, bf16[768,384]{1,0:T(8,128)(2,1)S(1)}, u32[]{:S(2)}, u32[]{:S(2)}) collective-permute-start(bf16[768,384]{1,0:T(8,128)(2,1)S(1)} %maximum_select_fusion.8), channel_id=1, source_target_pairs={{0,4},{4,0},{8,12},{12,8},{16,20},{20,16},{24,28},{28,24},{1,5},{5... | collective-permute-start | bytes 1769480 | tf_op jit(solution)/shard_map/ppermute | solution.py:350
  293.9 28.7 %collective-permute-start.53 = (bf16[768,384]{1,0:T(8,128)(2,1)S(1)}, bf16[768,384]{1,0:T(8,128)(2,1)}, u32[]{:S(2)}, u32[]{:S(2)}) collective-permute-start(bf16[768,384]{1,0:T(8,128)(2,1)S(1)} %maximum_select_fusion.7), channel_id=1, source_target_pairs={{0,4},{4,0},{8,12},{12,8},{16,20},{20,16},{24,28},{28,24},{1,5},{5... | collective-permute-start | bytes 1769480 | tf_op jit(solution)/shard_map/ppermute | solution.py:350
  299.9 8.5 %collective-permute-start.49 = (bf16[192,384]{1,0:T(8,128)(2,1)S(1)}, bf16[192,384]{1,0:T(8,128)(2,1)S(1)}, u32[]{:S(2)}, u32[]{:S(2)}) collective-permute-start(bf16[192,384]{1,0:T(8,128)(2,1)S(1)} %maximum_select_fusion.15), channel_id=1, source_target_pairs={{0,8},{4,12},{8,0},{12,4},{16,24},{20,28},{24,16},{28,20},{1,9},{5... | collective-permute-start | bytes 442376 | tf_op jit(solution)/shard_map/ppermute | solution.py:350
  308.6 24.8 %collective-permute-start.52 = (bf16[384,384]{1,0:T(8,128)(2,1)S(1)}, bf16[384,384]{1,0:T(8,128)(2,1)}, u32[]{:S(2)}, u32[]{:S(2)}) collective-permute-start(bf16[384,384]{1,0:T(8,128)(2,1)S(1)} %maximum_select_fusion.14), channel_id=1, source_target_pairs={{0,4},{4,0},{8,12},{12,8},{16,20},{20,16},{24,28},{28,24},{1,5},{5... | collective-permute-start | bytes 884744 | tf_op jit(solution)/shard_map/ppermute | solution.py:350
  308.8 24.7 %collective-permute-start.51 = (bf16[384,384]{1,0:T(8,128)(2,1)S(1)}, bf16[384,384]{1,0:T(8,128)(2,1)}, u32[]{:S(2)}, u32[]{:S(2)}) collective-permute-start(bf16[384,384]{1,0:T(8,128)(2,1)S(1)} %maximum_select_fusion.13), channel_id=1, source_target_pairs={{0,4},{4,0},{8,12},{12,8},{16,20},{20,16},{24,28},{28,24},{1,5},{5... | collective-permute-start | bytes 884744 | tf_op jit(solution)/shard_map/ppermute | solution.py:350
  (41 other events, 236.9 us)
